TPU v7x, 32 devices: a whole 2x2x4 slice. The times are simulated.
32 devices in a mesh: req: 8 (over z, x), mlp: 4 (over y, core).
Axes of the slice: x: 2, y: 2, z: 4, core: 2. Of those that a mesh axis runs over, the one named last changes fastest.
Arguments:
- x_pages: bfloat16 [256, 8, 4096], P('req', None, 'mlp'), may hold values from -6 to 6
- page_owner: int32 [256], P('req'), may hold values from 0 to 7, as said below
- request_id: int32 [2048], P('req'), may hold values from 0 to 2047, as said below
- adapter_table: int32 [2048], P('req'), may hold values from 0 to 63
- ln_gain: float32 [4096], replicated, may hold values from 0.5 to 1.5
- ln_bias: float32 [4096], replicated, may hold values from -3 to 3
- w_query: bfloat16 [4096, 2048], P('req', 'mlp'), may hold values from -0.09375 to 0.09375
- w_key: bfloat16 [4096, 2048], P('req', 'mlp'), may hold values from -0.09375 to 0.09375
- w_value: bfloat16 [4096, 2048], P('req', 'mlp'), may hold values from -0.09375 to 0.09375
- w_attn_out: bfloat16 [2048, 4096], P('mlp', 'req'), may hold values from -0.125 to 0.125
- down_query: bfloat16 [4096, 1024], P('mlp'), may hold values from -0.09375 to 0.09375
- up_query: bfloat16 [1024, 2048], P(None, 'mlp'), may hold values from -1.5 to 1.5
- down_value: bfloat16 [4096, 1024], P('mlp'), may hold values from -0.09375 to 0.09375
- up_value: bfloat16 [1024, 2048], P(None, 'mlp'), may hold values from -1.5 to 1.5
- w_fc_in: bfloat16 [4096, 8192], P('req', 'mlp'), may hold values from -0.09375 to 0.09375
- b_fc_in: float32 [8192], P('mlp'), may hold values from -3 to 3
- down_fc: bfloat16 [4096, 1024], P('mlp'), may hold values from -0.09375 to 0.09375
- up_fc: bfloat16 [1024, 8192], P(None, 'mlp'), may hold values from -1.5 to 1.5
- w_fc_out: bfloat16 [8192, 4096], P('mlp', 'req'), may hold values from -0.0625 to 0.0625
- b_fc_out: float32 [4096], P('mlp'), may hold values from -3 to 3
Outputs:
- out_pages: bfloat16 [256, 8, 4096], P('req', None, 'mlp')
Inputs may be any that keep to these rules, and one draw needn't show every extreme that they name: `page_owner`: every owner receives exactly 32 pages, at most 5 of them from one device, and some device sends exactly 5 pages to some owner. `request_id`: ids never fall; every request lies inside one owner's block of 256 rows, and the ids of block k lie in k * 256 to k * 256 + 255; some request is 256 long.
All inputs are finite; a program needn't handle non-finite values.
Results may differ from a plain program's by a relative error of at most 0.006.
Values may be sent and summed in bfloat16 or wider, within the bound.
A program may use at most 128 MiB of HBM per device.

v0:
```python
import jax
import jax.numpy as jnp
from jax import lax
from jax.sharding import PartitionSpec as P

HS = 256
ROT = 64
NAD = 64
R = 16


EPS = 1e-05


def gelu_tanh(v):
    return 0.5 * v * (1.0 + jnp.tanh(0.7978845608028654 * (v + 0.044715 * v * v * v)))


def rotate(block, pos):
    half = ROT // 2
    freq = jnp.power(10000.0, -jnp.arange(half).astype(jnp.float32) * 2.0 / ROT)
    angle = pos.astype(jnp.float32)[:, None, None] * freq[None, None, :]
    cosine = jnp.cos(angle)
    sine = jnp.sin(angle)
    even = block[:, :, 0:ROT:2]
    odd = block[:, :, 1:ROT:2]
    turned = jnp.stack([even * cosine - odd * sine, odd * cosine + even * sine], axis=-1)
    turned = turned.reshape(block.shape[0], block.shape[1], ROT)
    return jnp.concatenate([turned, block[:, :, ROT:]], axis=2)


def on_device(
    x_pages,
    page_owner,
    request_id,
    adapter_table,
    ln_gain,
    ln_bias,
    w_query,
    w_key,
    w_value,
    w_attn_out,
    down_query,
    up_query,
    down_value,
    up_value,
    w_fc_in,
    b_fc_in,
    down_fc,
    up_fc,
    w_fc_out,
    b_fc_out,
):
    groups = lax.axis_size("req")
    pg_dev = x_pages.shape[0]
    page_len = x_pages.shape[1]
    width_m = x_pages.shape[2]
    tok = request_id.shape[0]
    per_owner = pg_dev // groups + 1
    slots = groups * per_owner
    page_iota = jnp.arange(pg_dev)
    earlier = (page_owner[None, :] == page_owner[:, None]) & (
        page_iota[None, :] < page_iota[:, None]
    )
    rank = jnp.sum(earlier.astype(jnp.int32), axis=1)
    slot = page_owner * per_owner + rank
    place = (slot[None, :] == jnp.arange(slots)[:, None]).astype(jnp.bfloat16)
    flat_pages = x_pages.reshape(pg_dev, page_len * width_m)
    outgoing = jnp.dot(place, flat_pages, preferred_element_type=jnp.float32).astype(jnp.bfloat16)
    outgoing = outgoing.reshape(groups, per_owner, page_len * width_m)
    filled = jnp.sum(place, axis=1).reshape(groups, per_owner)
    arrived, marks = (
        lax.all_to_all(outgoing, "req", split_axis=0, concat_axis=0, tiled=True),
        lax.all_to_all(filled, "req", split_axis=0, concat_axis=0, tiled=True),
    )
    valid = marks.reshape(slots).astype(jnp.float32)
    position = jnp.cumsum(valid) - 1.0
    take = (
        (position[None, :] == jnp.arange(pg_dev).astype(jnp.float32)[:, None])
        & (valid[None, :] > 0.5)
    ).astype(jnp.bfloat16)
    own_x = jnp.dot(
        take, arrived.reshape(slots, page_len * width_m), preferred_element_type=jnp.float32
    )
    own_x = own_x.astype(jnp.bfloat16).reshape(tok, width_m)
    column = lax.axis_index("mlp") * width_m
    whole = lax.all_gather(own_x, "mlp", axis=1, tiled=True).astype(jnp.float32)
    mean = jnp.mean(whole, axis=1, keepdims=True)
    var = jnp.mean(jnp.square(whole - mean), axis=1, keepdims=True)
    full_ln = ((whole - mean) * lax.rsqrt(var + EPS) * ln_gain + ln_bias).astype(jnp.bfloat16)
    ln_m = lax.dynamic_slice_in_dim(full_ln, column, width_m, 1)
    local_req = request_id - lax.axis_index("req") * tok
    lookup = local_req[:, None] == jnp.arange(tok)[None, :]
    adapter = jnp.sum(jnp.where(lookup, adapter_table[None, :], 0), axis=1)
    onehot = (adapter[:, None] == jnp.arange(NAD)[None, :]).astype(jnp.float32)
    onehot_low = onehot.astype(jnp.bfloat16)

    def pick(down):
        spread = jnp.dot(ln_m, down, preferred_element_type=jnp.float32).reshape(tok, NAD, R)
        return jnp.sum(spread * onehot[:, :, None], axis=1)

    picked = lax.psum((pick(down_query), pick(down_value), pick(down_fc)), "mlp")

    def lift(chosen, up):
        expanded = (onehot_low[:, :, None] * chosen.astype(jnp.bfloat16)[:, None, :]).reshape(
            tok, NAD * R
        )
        return jnp.dot(expanded, up, preferred_element_type=jnp.float32)

    row_iota = jnp.arange(tok)
    start = jnp.sum((request_id[None, :] < request_id[:, None]).astype(jnp.int32), axis=1)
    pos = row_iota - start
    mask = (request_id[:, None] == request_id[None, :]) & (row_iota[None, :] <= row_iota[:, None])
    heads_w = w_query.shape[1]
    pieces = (
        lax.all_gather(w_query, "req", axis=0, tiled=True),
        lax.all_gather(w_key, "req", axis=0, tiled=True),
        lax.all_gather(w_value, "req", axis=0, tiled=True),
    )
    cols = full_ln
    base_q, base_k, base_v = tuple(
        [jnp.dot(cols, piece, preferred_element_type=jnp.float32) for piece in pieces]
    )
    query = rotate(
        (base_q + lift(picked[0], up_query)).reshape(tok, heads_w // HS, HS), pos
    ).astype(jnp.bfloat16)
    keys = rotate(base_k.reshape(tok, heads_w // HS, HS), pos).astype(jnp.bfloat16)
    value = (
        (base_v + lift(picked[1], up_value)).astype(jnp.bfloat16).reshape(tok, heads_w // HS, HS)
    )
    scores = jnp.einsum("qhd,khd->hqk", query, keys, preferred_element_type=jnp.float32) * HS ** (
        -0.5
    )
    scores = jnp.where(mask[None, :, :], scores, -1e30)
    top = jnp.max(scores, axis=2, keepdims=True)
    weights = jnp.exp(scores - top)
    probs = (weights / jnp.sum(weights, axis=2, keepdims=True)).astype(jnp.bfloat16)
    mixed_heads = jnp.einsum("hqk,khd->qhd", probs, value, preferred_element_type=jnp.float32)
    attn = mixed_heads.astype(jnp.bfloat16).reshape(tok, heads_w)
    cols = full_ln
    hidden_pre = jnp.dot(
        cols, lax.all_gather(w_fc_in, "req", axis=0, tiled=True), preferred_element_type=jnp.float32
    )
    hidden_pre = hidden_pre + lift(picked[2], up_fc) + b_fc_in
    hidden = gelu_tanh(hidden_pre).astype(jnp.bfloat16)
    pieces = (
        lax.all_gather(w_attn_out, "req", axis=1, tiled=True),
        lax.all_gather(w_fc_out, "req", axis=1, tiled=True),
    )
    part = jnp.dot(attn, pieces[0], preferred_element_type=jnp.float32) + jnp.dot(
        hidden, pieces[1], preferred_element_type=jnp.float32
    )
    shares = lax.psum_scatter(part, "mlp", scatter_dimension=1, tiled=True)
    result = (own_x.astype(jnp.float32) + shares + b_fc_out).astype(jnp.bfloat16)
    back_flat = result.reshape(pg_dev, page_len * width_m)
    leaving = jnp.dot(take.T, back_flat, preferred_element_type=jnp.float32).astype(jnp.bfloat16)
    leaving = leaving.reshape(groups, per_owner, page_len * width_m)
    returned = lax.all_to_all(leaving, "req", split_axis=0, concat_axis=0, tiled=True)
    pages_back = jnp.dot(
        place.T, returned.reshape(slots, page_len * width_m), preferred_element_type=jnp.float32
    )
    return pages_back.astype(jnp.bfloat16).reshape(pg_dev, page_len, width_m)


def solution(mesh):
    in_specs = (
        P("req", None, "mlp"),
        P("req"),
        P("req"),
        P("req"),
        P(),
        P(),
        P("req", "mlp"),
        P("req", "mlp"),
        P("req", "mlp"),
        P("mlp", "req"),
        P("mlp", None),
        P(None, "mlp"),
        P("mlp", None),
        P(None, "mlp"),
        P("req", "mlp"),
        P("mlp"),
        P("mlp", None),
        P(None, "mlp"),
        P("mlp", "req"),
        P("mlp"),
    )
    out_specs = P("req", None, "mlp")
    return jax.shard_map(
        on_device, mesh=mesh, in_specs=in_specs, out_specs=out_specs, check_vma=False
    )
```

profile of v0, /device:TPU:0, one launch (start us, length us, event | category | flops | bytes accessed | tf_op | source)
XLA Modules:
  0.0 923.4 jit_solution(5489891884460698850)
XLA Ops:
  9.0 7.3 all-to-all-start
  19.3 3.3 all-to-all-done
  22.6 3.6 all-to-all-start.1
  26.6 24.3 %all-to-all-done.1 = bf16[8,5,8192]{2,1,0:T(8,128)(2,1)S(1)} async-done(((bf16[8,5,8192]{2,1,0:T(8,128)(2,1)}), bf16[8,5,8192]{2,1,0:T(8,128)(2,1)S(1)}, u32[]{:S(2)}, u32[]{:S(2)}) %all-to-all-start.1) | async-done | bytes 655392 | tf_op jit(solution)/shard_map/all_to_all | solution.py:73
  52.1 1.4 convolution_convert_fusion.3
  59.9 16.3 %all-gather.8.cloned.1.call-done = bf16[256,4096]{1,0:T(8,128)(2,1)} async-done(((bf16[256,1024]{1,0:T(8,128)(2,1)}), bf16[256,4096]{1,0:T(8,128)(2,1)}) %all-gather.8.cloned.1.call-update) | async-done | bytes 2097168 | tf_op jit(solution)/shard_map/all_gather | solution.py:87
  76.2 2.1 convert_reduce_fusion
  81.2 1.4 copy-done.6
  85.5 11.7 %all-reduce = (bf16[256,16]{0,1:T(8,128)(2,1)S(1)}, bf16[256,16]{0,1:T(8,128)(2,1)S(1)}, bf16[256,16]{0,1:T(8,128)(2,1)S(1)}) all-reduce(f32[256,16]{0,1:T(8,128)S(1)} %get-tuple-element.6, f32[256,16]{0,1:T(8,128)S(1)} %get-tuple-element.7, f32[256,16]{0,1:T(8,128)S(1)} %get-tuple-element.5), channel_id=1, replica_groups=mesh['req'=8,'mlp'=4] {'mlp'}, use_global_device_ids=true, to_apply=%region_14.15 | all-reduce | flops 12288 | bytes 73728 | tf_op jit(solution)/shard_map/psum | solution.py:102
  98.3 53.4 %all-gather.12.cloned.1.call-done = bf16[4096,512]{1,0:T(8,128)(2,1)} async-done(((bf16[512,512]{1,0:T(8,128)(2,1)}), bf16[4096,512]{1,0:T(8,128)(2,1)}) %all-gather.12.cloned.1.call-update) | async-done | bytes 4194320 | tf_op jit(solution)/shard_map/all_gather | solution.py:116
  151.7 3.5 fusion.77
  156.1 5.2 slice.20
  161.3 4.1 slice.21
  165.3 60.2 %all-gather.14.cloned.1.call-done = bf16[4096,512]{1,0:T(8,128)(2,1)} async-done(((bf16[512,512]{1,0:T(8,128)(2,1)}), bf16[4096,512]{1,0:T(8,128)(2,1)}) %all-gather.14.cloned.1.call-update) | async-done | bytes 4194320 | tf_op jit(solution)/shard_map/all_gather | solution.py:117
  225.6 4.2 fusion.78
  229.8 1.4 reshape.308
  231.2 5.2 slice.23
  236.4 5.2 slice.24
  247.8 51.5 %all-gather.10.cloned.1.call-done = bf16[4096,512]{1,0:T(8,128)(2,1)} async-done(((bf16[512,512]{1,0:T(8,128)(2,1)}), bf16[4096,512]{1,0:T(8,128)(2,1)}) %all-gather.10.cloned.1.call-update) | async-done | bytes 4194320 | tf_op jit(solution)/shard_map/all_gather | solution.py:118
  299.3 3.5 fusion.76
  303.4 1.4 fusion.71
  306.0 1.7 convolution_convert_fusion.4
  307.7 219.4 %all-gather.18.cloned.1.call-done = bf16[4096,2048]{1,0:T(8,128)(2,1)} async-done(((bf16[512,2048]{1,0:T(8,128)(2,1)}), bf16[4096,2048]{1,0:T(8,128)(2,1)}) %all-gather.18.cloned.1.call-update) | async-done | bytes 16777232 | tf_op jit(solution)/shard_map/all_gather | solution.py:142
  527.1 9.4 %fusion.79 = f32[256,2048]{1,0:T(8,128)} fusion(bf16[256,4096]{1,0:T(8,128)(2,1)S(1)} %copy-done.4, bf16[4096,2048]{1,0:T(8,128)(2,1)} %all-gather.18.cloned.1.call-done), kind=kOutput, calls=%fused_computation.120 | convolution fusion | flops 4294967296 | bytes 20971520 | tf_op jit(solution)/shard_map/dot_general | solution.py:141
  536.5 218.5 %all-gather.20.cloned.1.call-done = bf16[2048,4096]{1,0:T(8,128)(2,1)} async-done(((bf16[2048,512]{1,0:T(8,128)(2,1)}), bf16[2048,4096]{1,0:T(8,128)(2,1)}) %all-gather.20.cloned.1.call-update) | async-done | bytes 16777232 | tf_op jit(solution)/shard_map/all_gather | solution.py:148
  755.0 14.2 %fusion.13 = f32[256,4096]{1,0:T(8,128)} fusion(bf16[2048,4096]{1,0:T(8,128)(2,1)} %all-gather.20.cloned.1.call-done, f32[256,2048]{1,0:T(8,128)} %fusion.79, bf16[256,1024]{0,1:T(8,128)(2,1)S(1)} %bitcast.63, bf16[1024,2048]{1,0:T(8,128)(2,1)} %param.37, f32[2048]{0:T(1024)S(1)} %copy-done.20), kind=kOutput, calls=%fused_computation.22 | convolution fusion | flops 5374476288 | bytes 27795456 | tf_op jit(solution)/shard_map/dot_general | solution.py:150
  769.2 61.1 %all-gather.16.cloned.1.call-done = bf16[512,4096]{1,0:T(8,128)(2,1)} async-done(((bf16[512,512]{1,0:T(8,128)(2,1)}), bf16[512,4096]{1,0:T(8,128)(2,1)}) %all-gather.16.cloned.1.call-update) | async-done | bytes 4194320 | tf_op jit(solution)/shard_map/all_gather | solution.py:147
  830.3 6.7 convolution_add_fusion
  837.0 42.8 %reduce-scatter.2.cloned.1.call-done = f32[256,1024]{1,0:T(8,128)} async-done(((f32[256,4096]{1,0:T(8,128)}), f32[256,1024]{1,0:T(8,128)}) %reduce-scatter.2.cloned.1.call-update) | async-done | bytes 1048592 | tf_op jit(solution)/shard_map/reduce_scatter | solution.py:153
  879.9 1.4 add_convert_fusion
  882.3 31.3 %all_to_all.20 = bf16[8,5,8192]{2,1,0:T(8,128)(2,1)} all-to-all(bf16[8,5,8192]{2,1,0:T(8,128)(2,1)S(1)} %reshape.313), channel_id=1, replica_groups=mesh['req'=8,'mlp'=4] {'req'}, dimensions={0} | all-to-all | bytes 1310720 | tf_op jit(solution)/shard_map/all_to_all | solution.py:158
  913.6 1.5 reshape.314
  (114 shorter events, 31.3 us)
Async XLA Ops:
  6.5 73.6 %copy-start = (bf16[1024,1024]{1,0:T(8,128)(2,1)S(1)}, bf16[1024,1024]{1,0:T(8,128)(2,1)}, u32[]{:S(2)}) copy-start(bf16[1024,1024]{1,0:T(8,128)(2,1)} %param.32) | copy-start | bytes 6291460
  9.0 13.6 %all-to-all-start = ((bf16[8,1,5]{2,1,0:T(2,128)(2,1)}), bf16[8,1,5]{2,1,0:T(2,128)(2,1)S(1)}, u32[]{:S(2)}, u32[]{:S(2)}) async-start(bf16[8,1,5]{2,1,0:T(2,128)(2,1)} %all_to_all.16), calls=%async_computation | async-start | bytes 8192 | tf_op jit(solution)/shard_map/all_to_all | solution.py:74
  22.6 28.3 %all-to-all-start.1 = ((bf16[8,5,8192]{2,1,0:T(8,128)(2,1)}), bf16[8,5,8192]{2,1,0:T(8,128)(2,1)S(1)}, u32[]{:S(2)}, u32[]{:S(2)}) async-start(bf16[8,5,8192]{2,1,0:T(8,128)(2,1)} %reshape.300), calls=%async_computation.1 | async-start | bytes 2097152 | tf_op jit(solution)/shard_map/all_to_all | solution.py:73
  26.2 50.0 %all-gather.8.cloned.1.call-start = ((), (), s32[]{:S(2)}) async-start(), calls=%async_computation.4 | async-start | bytes 2621440 | tf_op jit(solution)/shard_map/all_gather | solution.py:87
  54.6 97.2 %all-gather.12.cloned.1.call-start = ((), (), s32[]{:S(2)}) async-start(), calls=%async_computation.6 | async-start | bytes 4718592 | tf_op jit(solution)/shard_map/all_gather | solution.py:116
  55.3 170.3 %all-gather.14.cloned.1.call-start = ((), (), s32[]{:S(2)}) async-start(), calls=%async_computation.7 | async-start | bytes 4718592 | tf_op jit(solution)/shard_map/all_gather | solution.py:117
  56.0 243.2 %all-gather.10.cloned.1.call-start = ((), (), s32[]{:S(2)}) async-start(), calls=%async_computation.5 | async-start | bytes 4718592 | tf_op jit(solution)/shard_map/all_gather | solution.py:118
  56.6 2.0 copy-start.15
  56.6 2.8 copy-start.19
  56.6 470.5 %all-gather.18.cloned.1.call-start = ((), (), s32[]{:S(2)}) async-start(), calls=%async_computation.9 | async-start | bytes 18874368 | tf_op jit(solution)/shard_map/all_gather | solution.py:142
  57.2 697.8 %all-gather.20.cloned.1.call-start = ((), (), s32[]{:S(2)}) async-start(), calls=%async_computation.10 | async-start | bytes 18874368 | tf_op jit(solution)/shard_map/all_gather | solution.py:148
  57.8 772.5 %all-gather.16.cloned.1.call-start = ((), (), s32[]{:S(2)}) async-start(), calls=%async_computation.8 | async-start | bytes 4718592 | tf_op jit(solution)/shard_map/all_gather | solution.py:147
  58.6 821.3 %reduce-scatter.2.cloned.1.call-start = ((), (), s32[]{:S(2)}) async-start(), calls=%async_computation.11 | async-start | bytes 5242880 | tf_op jit(solution)/shard_map/reduce_scatter | solution.py:153
  76.2 2.2 copy-start.2
  76.2 2.9 copy-start.16
  76.2 2.9 copy-start.17
  80.2 3.3 copy-start.3
  80.2 2.4 copy-start.6
  82.5 1.6 copy-start.7
  85.1 66.7 %copy-start.4 = (bf16[256,4096]{1,0:T(8,128)(2,1)S(1)}, bf16[256,4096]{1,0:T(8,128)(2,1)}, u32[]{:S(2)}) copy-start(bf16[256,4096]{1,0:T(8,128)(2,1)} %copy-done.3) | copy-start | bytes 6291460
  151.7 3.5 copy-start.9
  242.7 5.0 copy-start.11
  247.7 55.0 %copy-start.8 = (bf16[256,64,16]{0,2,1:T(8,128)(2,1)S(1)}, bf16[256,64,16]{0,2,1:T(8,128)(2,1)}, u32[]{:S(2)}) copy-start(bf16[256,64,16]{0,2,1:T(8,128)(2,1)} %get-tuple-element.19) | copy-start | bytes 1572868
  299.2 3.5 copy-start.10
  303.3 1.5 copy-start.13
  303.3 1.5 copy-start.14
  307.7 447.3 %copy-start.12 = (bf16[256,64,16]{0,2,1:T(8,128)(2,1)S(1)}, bf16[256,64,16]{0,2,1:T(8,128)(2,1)}, u32[]{:S(2)}) copy-start(bf16[256,64,16]{0,2,1:T(8,128)(2,1)} %get-tuple-element.18) | copy-start | bytes 1572868
  307.7 447.3 %copy-start.20 = (f32[2048]{0:T(1024)S(1)}, f32[2048]{0:T(1024)}, u32[]{:S(2)}) copy-start(f32[2048]{0:T(1024)} %param.35) | copy-start | bytes 24580
  837.0 42.9 %copy-start.5 = (bf16[256,1024]{1,0:T(8,128)(2,1)S(1)}, bf16[256,1024]{1,0:T(8,128)(2,1)}, u32[]{:S(2)}) copy-start(bf16[256,1024]{1,0:T(8,128)(2,1)} %reshape.302) | copy-start | bytes 1572868
  837.0 42.9 %copy-start.18 = (f32[1024]{0:T(1024)S(1)}, f32[1024]{0:T(1024)}, u32[]{:S(2)}) copy-start(f32[1024]{0:T(1024)} %param.39) | copy-start | bytes 12292
  882.3 34.3 %copy-start.1 = (bf16[1024,1024]{1,0:T(8,128)(2,1)S(1)}, bf16[1024,1024]{1,0:T(8,128)(2,1)}, u32[]{:S(2)}) copy-start(bf16[1024,1024]{1,0:T(8,128)(2,1)} %param.32) | copy-start | bytes 6291460
Sparse Core Ops, SparseCore 0:
  54.7 21.4 all-gather.7
  78.3 73.3 all-gather.11
  153.9 71.6 all-gather.13
  227.5 71.6 all-gather.9
  301.2 225.8 all-gather.17
  529.0 225.9 all-gather.19
  757.0 73.1 all-gather.15
  837.1 42.6 reduce-scatter.1
where the time goes:
time: 924 us; the launch traced here: 923 us
  waiting for transfers between devices  755 us (82%)
  matrix products  52.3 us (6%)
  blocking collectives  43 us (5%)
  local copies, waits for them, and re-layouts  38.2 us (4%)
  between operations  14 us (2%)
  starting transfers between devices  11.1 us (1%)
  other arithmetic  10.3 us (1%)
    all_gather x1, waiting for transfers between devices, on_device(): lax.all_gather(w_fc_in, 'req', axis=0, tiled=True)  219 us
    all_gather x1, waiting for transfers between devices, on_device(): lax.all_gather(w_fc_out, 'req', axis=1, tiled=True)  218 us
    all_gather x1, waiting for transfers between devices, on_device(): lax.all_gather(w_attn_out, 'req', axis=1, tiled=True)  61.1 us
    all_gather x1, waiting for transfers between devices, on_device(): lax.all_gather(w_key, 'req', axis=0, tiled=True)  60.2 us
    all_gather x1, waiting for transfers between devices, on_device(): lax.all_gather(w_query, 'req', axis=0, tiled=True)  53.4 us
    all_gather x1, waiting for transfers between devices, on_device(): lax.all_gather(w_value, 'req', axis=0, tiled=True)  51.5 us
    reduce_scatter x1, waiting for transfers between devices, on_device(): shares = lax.psum_scatter(part, 'mlp', scatter_dimension=1, tiled=True)  42.8 us
    all_to_all x1, blocking collectives, on_device(): lax.all_to_all(leaving, 'req', split_axis=0, concat_axis=0, tiled=True)  31.3 us
  transfers between devices with their start and end apart: 10, of which 10 were waited for; matrix products, arithmetic and copies ran while one was open for 9% of the time, Pallas kernels for 0%

commit v1 on v0

v1 whole, which is shorter than its diff:
```python
import jax
import jax.numpy as jnp
from jax import lax
from jax.sharding import PartitionSpec as P

HS = 256
ROT = 64
NAD = 64
R = 16
EPS = 1e-05

bf16 = jnp.bfloat16
f32 = jnp.float32


def mm(a, b):
    return jnp.dot(a, b, preferred_element_type=f32)


def gelu_tanh(v):
    return 0.5 * v * (1.0 + jnp.tanh(0.7978845608028654 * (v + 0.044715 * v * v * v)))


def rotate_flat(block, pos):
    cols = block.shape[1]
    within = jnp.arange(cols) % HS
    turned = within < ROT
    freq = jnp.power(10000.0, -(within // 2).astype(f32) * 2.0 / ROT)
    angle = jnp.where(turned[None, :], pos.astype(f32)[:, None] * freq[None, :], 0.0)
    even = (within % 2 == 0)[None, :]
    other = jnp.where(even, -jnp.roll(block, -1, axis=1), jnp.roll(block, 1, axis=1))
    return jnp.where(turned[None, :], block * jnp.cos(angle) + other * jnp.sin(angle), block)


def scatter_sum(part):
    return lax.psum_scatter(part, "req", scatter_dimension=0, tiled=False)


def gather_rows(act):
    return lax.all_gather(act, "req", axis=0, tiled=False)


def on_device(
    x_pages,
    page_owner,
    request_id,
    adapter_table,
    ln_gain,
    ln_bias,
    w_query,
    w_key,
    w_value,
    w_attn_out,
    down_query,
    up_query,
    down_value,
    up_value,
    w_fc_in,
    b_fc_in,
    down_fc,
    up_fc,
    w_fc_out,
    b_fc_out,
):
    groups = lax.axis_size("req")
    lanes = lax.axis_size("mlp")
    me = lax.axis_index("req")
    pg_dev, page_len, width_m = x_pages.shape
    pages = groups * pg_dev
    tok = request_id.shape[0]
    width = width_m * lanes
    chunk = w_query.shape[0]
    heads_w = w_query.shape[1]
    ff = w_fc_in.shape[1]

    local_req = request_id - me * tok
    lookup = local_req[:, None] == jnp.arange(tok)[None, :]
    adapter = jnp.sum(jnp.where(lookup, adapter_table[None, :], 0), axis=1)
    ints = lax.all_gather(jnp.concatenate([page_owner, adapter]), "req", axis=0, tiled=False)
    owner_all = ints[:, :pg_dev].reshape(pages)
    adapter_all = ints[:, pg_dev:].reshape(pages, page_len)
    iota = jnp.arange(pages)
    earlier = (owner_all[None, :] == owner_all[:, None]) & (iota[None, :] < iota[:, None])
    dest = owner_all * pg_dev + jnp.sum(earlier.astype(jnp.int32), axis=1)
    perm = dest[None, :] == iota[:, None]
    perm_low = perm.astype(bf16)
    mine = lax.dynamic_slice_in_dim(dest, me * pg_dev, pg_dev, 0)
    held_adapter = jnp.sum(
        jnp.where((mine[:, None] == iota[None, :])[:, :, None], adapter_all[None, :, :], 0), axis=1
    ).reshape(tok)

    x = x_pages.reshape(tok, width_m).astype(f32)
    local_mean = jnp.mean(x, axis=1)
    local_m2 = jnp.sum(jnp.square(x - local_mean[:, None]), axis=1)
    stats = lax.all_gather(jnp.stack([local_mean, local_m2]), "mlp", axis=0, tiled=False)
    mean = jnp.mean(stats[:, 0], axis=0)
    m2 = jnp.sum(stats[:, 1] + width_m * jnp.square(stats[:, 0] - mean[None, :]), axis=0)
    scale = lax.rsqrt(m2 / width + EPS)
    column = lax.axis_index("mlp") * width_m
    gain = lax.dynamic_slice_in_dim(ln_gain, column, width_m, 0)
    bias = lax.dynamic_slice_in_dim(ln_bias, column, width_m, 0)
    normed = ((x - mean[:, None]) * scale[:, None] * gain + bias).astype(bf16)

    full_rows = lax.all_gather(normed, "mlp", axis=1, tiled=True)
    everyone = lax.all_to_all(full_rows, "req", split_axis=1, concat_axis=0, tiled=True)
    ordered = mm(perm_low, everyone.reshape(pages, page_len * chunk)).astype(bf16)
    ordered = ordered.reshape(groups * tok, chunk)

    col_adapter = jnp.arange(NAD * R) // R
    fold = (jnp.arange(NAD * R)[:, None] % R == jnp.arange(R)[None, :]).astype(bf16)
    held_mask = held_adapter[:, None] == col_adapter[None, :]

    def pick(down):
        return mm(jnp.where(held_mask, mm(normed, down), 0.0).astype(bf16), fold)

    picked = jnp.concatenate([pick(down_query), pick(down_value), pick(down_fc)], axis=1)
    picked = lax.all_gather(picked.astype(bf16), ("req", "mlp"), axis=0, tiled=False)
    picked = jnp.sum(picked.reshape(groups, lanes, tok, 3 * R).astype(f32), axis=1).astype(bf16)
    own_perm = lax.dynamic_slice_in_dim(perm_low, me * pg_dev, pg_dev, 0)
    chosen = mm(own_perm, picked.reshape(pages, page_len * 3 * R)).astype(bf16)
    chosen = chosen.reshape(tok, 3 * R)
    own_mask = adapter[:, None] == col_adapter[None, :]

    def lift(low, up):
        wide = mm(low, fold.T).astype(bf16)
        return mm(jnp.where(own_mask, wide, jnp.zeros((), bf16)), up)

    part = jnp.concatenate(
        [mm(ordered, w).astype(bf16) for w in (w_query, w_key, w_value, w_fc_in)], axis=1
    )
    base = scatter_sum(part.reshape(groups, tok, 3 * heads_w + ff)).astype(f32)

    row_iota = jnp.arange(tok)
    start = jnp.sum((request_id[None, :] < request_id[:, None]).astype(jnp.int32), axis=1)
    pos = row_iota - start
    mask = (request_id[:, None] == request_id[None, :]) & (row_iota[None, :] <= row_iota[:, None])
    query = base[:, :heads_w] + lift(chosen[:, :R], up_query)
    query = rotate_flat(query, pos).astype(bf16).reshape(tok, heads_w // HS, HS)
    keys = rotate_flat(base[:, heads_w : 2 * heads_w], pos).astype(bf16)
    keys = keys.reshape(tok, heads_w // HS, HS)
    value = base[:, 2 * heads_w : 3 * heads_w] + lift(chosen[:, R : 2 * R], up_value)
    value = value.astype(bf16).reshape(tok, heads_w // HS, HS)
    scores = jnp.einsum("qhd,khd->hqk", query, keys, preferred_element_type=f32) * HS ** (-0.5)
    scores = jnp.where(mask[None, :, :], scores, -1e30)
    top = jnp.max(scores, axis=2, keepdims=True)
    weights = jnp.exp(scores - top)
    probs = (weights / jnp.sum(weights, axis=2, keepdims=True)).astype(bf16)
    attn = jnp.einsum("hqk,khd->qhd", probs, value, preferred_element_type=f32)
    attn = attn.astype(bf16).reshape(tok, heads_w)
    hidden = gelu_tanh(base[:, 3 * heads_w :] + lift(chosen[:, 2 * R :], up_fc) + b_fc_in)
    act = jnp.concatenate([attn, hidden.astype(bf16)], axis=1)

    acts = gather_rows(act).reshape(groups * tok, heads_w + ff)
    out = mm(acts[:, :heads_w], w_attn_out) + mm(acts[:, heads_w:], w_fc_out)
    out = out.astype(bf16).reshape(pages, page_len * chunk)
    out = mm(perm_low.T, out).astype(bf16).reshape(groups * tok, chunk)
    shares = lax.all_to_all(out, "req", split_axis=0, concat_axis=1, tiled=True)
    shares = lax.psum_scatter(shares, "mlp", scatter_dimension=1, tiled=True)
    result = (x + shares.astype(f32) + b_fc_out).astype(bf16)
    return result.reshape(pg_dev, page_len, width_m)


def solution(mesh):
    in_specs = (
        P("req", None, "mlp"),
        P("req"),
        P("req"),
        P("req"),
        P(),
        P(),
        P("req", "mlp"),
        P("req", "mlp"),
        P("req", "mlp"),
        P("mlp", "req"),
        P("mlp", None),
        P(None, "mlp"),
        P("mlp", None),
        P(None, "mlp"),
        P("req", "mlp"),
        P("mlp"),
        P("mlp", None),
        P(None, "mlp"),
        P("mlp", "req"),
        P("mlp"),
    )
    out_specs = P("req", None, "mlp")
    return jax.shard_map(
        on_device, mesh=mesh, in_specs=in_specs, out_specs=out_specs, check_vma=False
    )
```

time: 924 us -> 699 us (0.76)
  waiting for transfers between devices: 755 us -> 386 us
  blocking collectives: 43 us -> 173 us
  other arithmetic: 10.3 us -> 23.2 us
  local copies, waits for them, and re-layouts: 38.2 us -> 50.8 us
    all_gather x7 -> x2, waiting for transfers between devices: 680 us -> 174 us  [the longest x1 150 us: gather_rows(): return lax.all_gather(act, 'req', axis=0, tiled=False)]
    reduce_scatter x1 -> x2, waiting for transfers between devices: 42.8 us -> 211 us  [the longest x1 181 us: scatter_sum(): return lax.psum_scatter(part, 'req', scatter_dimension=0, tiled=False)]
    unnamed x0 -> x1, blocking collectives: none -> 70.2 us
    all_gather x0 -> x2, blocking collectives: none -> 51 us  [the longest x1 44.9 us: on_device(): lax.all_gather(picked.astype(bf16), ('req', 'mlp'), axis=0, tiled=False)]
    all_to_all x2 -> x1, waiting for transfers between devices: 27.6 us -> 0.01 us  [on_device(): lax.all_to_all(full_rows, 'req', split_axis=1, concat_axis=0, tiled=True)]
    reshape x11 -> x9, local copies, waits for them, and re-layouts: 8.28 us -> 31.4 us  [the longest x1 18.8 us: on_device(): base = scatter_sum(part.reshape(groups, tok, 3 * heads_w + ff)).astype(f32)]
    all_to_all x1, blocking collectives: 31.3 us -> 51.3 us  [on_device(): shares = lax.all_to_all(out, 'req', split_axis=0, concat_axis=1, tiled=True)]
    slice x6, local copies, waits for them, and re-layouts: 21.1 us -> 2.09 us  [the longest x4 2.01 us: rotate_flat(): jnp.roll(block, 1, axis=1)]
  transfers between devices with their start and end apart: 10 -> 5, of which waited for: 10 -> 4; matrix products, arithmetic and copies ran while one was open for 9% -> 2% of each run, Pallas kernels for 0% -> 0%
where the time goes in v1:
time: 699 us; the launch traced here: 698 us
  waiting for transfers between devices  386 us (55%)
  blocking collectives  173 us (25%)
  local copies, waits for them, and re-layouts  50.8 us (7%)
  matrix products  45 us (6%)
  other arithmetic  23.2 us (3%)
  between operations  14.2 us (2%)
    reduce_scatter x1, waiting for transfers between devices, scatter_sum(): return lax.psum_scatter(part, 'req', scatter_dimension=0, tiled=False)  181 us
    all_gather x1, waiting for transfers between devices, gather_rows(): return lax.all_gather(act, 'req', axis=0, tiled=False)  150 us
    unnamed x1, blocking collectives  70.2 us
    all_to_all x1, blocking collectives, on_device(): shares = lax.all_to_all(out, 'req', split_axis=0, concat_axis=1, tiled=True)  51.3 us
    all_gather x1, blocking collectives, on_device(): lax.all_gather(picked.astype(bf16), ('req', 'mlp'), axis=0, tiled=False)  44.9 us
    dot_general x15, matrix products, mm(): return jnp.dot(a, b, preferred_element_type=f32)  44.4 us
    reduce_scatter x1, waiting for transfers between devices, on_device(): shares = lax.psum_scatter(shares, 'mlp', scatter_dimension=1, tiled=True)  30.6 us
    all_gather x1, waiting for transfers between devices, on_device(): full_rows = lax.all_gather(normed, 'mlp', axis=1, tiled=True)  24.5 us
  transfers between devices with their start and end apart: 5, of which 4 were waited for; matrix products, arithmetic and copies ran while one was open for 2% of the time, Pallas kernels for 0%

profile of v1, /device:TPU:0, one launch (start us, length us, event | category | flops | bytes accessed | tf_op | source)
XLA Modules:
  0.0 697.7 jit_solution(9910042820084681341)
XLA Ops:
  10.8 6.1 all-gather.3
  17.0 2.1 fusion.35
  19.1 24.5 %all-gather.7.cloned.1.call-done = bf16[256,4096]{1,0:T(8,128)(2,1)} async-done(((bf16[256,1024]{1,0:T(8,128)(2,1)}), bf16[256,4096]{1,0:T(8,128)(2,1)}) %all-gather.7.cloned.1.call-update) | async-done | bytes 2097168 | tf_op jit(solution)/shard_map/all_gather | solution.py:104
  43.6 3.1 copy.96
  46.7 5.7 all-to-all-start
  54.1 70.2 %all-reduce = s32[2304]{0:T(1024)S(1)} all-reduce(s32[2304]{0:T(1024)S(1)} %add_dynamic-update-slice_fusion), channel_id=2, replica_groups=mesh['req'=8,'mlp'=4] {'req'}, use_global_device_ids=true, to_apply=%add | all-reduce | flops 2304 | bytes 18432
  124.6 4.2 reshape.301
  128.8 3.7 convolution_convert_fusion.2
  132.5 4.2 reshape.302
  136.7 3.1 convolution_convert_fusion.3
  142.5 4.8 convolution_convert_fusion
  147.3 7.0 %pad_maximum_fusion = bf16[2048,3584]{0,1:T(8,128)(2,1)} fusion(bf16[2048,2048]{0,1:T(8,128)(2,1)S(1)} %convolution_convert_fusion, bf16[2048,512]{0,1:T(8,128)(2,1)S(1)} %convolution_convert_fusion.3, bf16[2048,512]{0,1:T(8,128)(2,1)S(1)} %convolution_convert_fusion.4, bf16[2048,512]{0,1:T(8,128)(2,1)S(1)} %convolution_convert_fusion.5), kind=kLoop, calls=%fused_computation.1 | loop fusion | flops 58720256 | bytes 29360128 | tf_op jit(solution)/shard_map/concatenate | solution.py:128
  154.3 18.8 %copy.73 = bf16[2048,3584]{1,0:T(8,128)(2,1)} copy(bf16[2048,3584]{0,1:T(8,128)(2,1)} %pad_maximum_fusion) | data formatting | bytes 29360128 | tf_op jit(solution)/shard_map/reshape | solution.py:131
  174.5 2.5 fusion.29
  177.0 2.8 fusion.30
  179.8 2.5 fusion.31
  182.3 44.9 %all_gather.30 = bf16[32,256,48]{1,2,0:T(8,128)(2,1)S(1)} all-gather(bf16[1,256,48]{1,2,0:T(8,128)(2,1)S(1)} %pad_maximum_fusion.2), channel_id=1, replica_groups=mesh['req'=8,'mlp'=4] {'req','mlp'}, dimensions={0}, use_global_device_ids=true | all-gather | bytes 811008 | tf_op jit(solution)/shard_map/all_gather | solution.py:117
  229.1 180.9 %reduce-scatter.3.cloned.1.call-done = bf16[1,256,3584]{2,1,0:T(8,128)(2,1)} async-done(((bf16[8,256,3584]{2,1,0:T(8,128)(2,1)}), bf16[1,256,3584]{2,1,0:T(8,128)(2,1)}) %reduce-scatter.3.cloned.1.call-update) | async-done | bytes 1835024 | tf_op jit(solution)/shard_map/reduce_scatter | solution.py:36
  417.5 2.8 fusion.25
  421.4 3.8 fusion.45
  426.2 5.0 fusion.8
  432.6 149.8 %all-gather.9.cloned.1.call-done = bf16[2048,2560]{1,0:T(8,128)(2,1)} async-done(((bf16[256,2560]{1,0:T(8,128)(2,1)}), bf16[2048,2560]{1,0:T(8,128)(2,1)}) %all-gather.9.cloned.1.call-update) | async-done | bytes 10485776 | tf_op jit(solution)/shard_map/all_gather | solution.py:40
  582.5 7.5 %fusion.1 = f32[2048,512]{1,0:T(8,128)S(1)} fusion(bf16[2048,512]{1,0:T(8,128)(2,1)} %param.38, bf16[2048,2560]{1,0:T(8,128)(2,1)} %all-gather.9.cloned.1.call-done), kind=kOutput, calls=%fused_computation.2 | convolution fusion | flops 4294967296 | bytes 14680064 | tf_op jit(solution)/shard_map/dot_general | solution.py:17
  590.0 2.9 add_convert_fusion
  593.0 2.4 reshape.312
  595.3 2.3 convolution_convert_fusion.1
  597.7 2.4 all_to_all.29
  600.1 2.8 copy.70
  602.9 51.3 %all_to_all.35 = bf16[8,256,512]{1,2,0:T(8,128)(2,1)} all-to-all(bf16[8,256,512]{1,2,0:T(8,128)(2,1)S(1)} %copy.70), channel_id=1, replica_groups=mesh['req'=8,'mlp'=4] {'req'}, dimensions={0} | all-to-all | bytes 4194304 | tf_op jit(solution)/shard_map/all_to_all | solution.py:157
  654.3 4.3 copy.71
  658.6 30.6 %reduce-scatter.5.cloned.1.call-done = bf16[256,1024]{1,0:T(8,128)(2,1)} async-done(((bf16[256,4096]{1,0:T(8,128)(2,1)}), bf16[256,1024]{1,0:T(8,128)(2,1)}) %reduce-scatter.5.cloned.1.call-update) | async-done | bytes 524304 | tf_op jit(solution)/shard_map/reduce_scatter | solution.py:158
  689.1 2.0 fusion.40
  (105 shorter events, 22.5 us)
Async XLA Ops:
  6.5 135.9 %copy-start = (bf16[512,2048]{1,0:T(8,128)(2,1)S(1)}, bf16[512,2048]{1,0:T(8,128)(2,1)}, u32[]{:S(2)}) copy-start(bf16[512,2048]{1,0:T(8,128)(2,1)} %param.34) | copy-start | bytes 6291460
  6.5 37.1 %all-gather.7.cloned.1.call-start = ((), (), s32[]{:S(2)}) async-start(), calls=%async_computation.4 | async-start | bytes 2621440 | tf_op jit(solution)/shard_map/all_gather | solution.py:104
  46.7 5.7 copy-start.19
  46.7 6.9 copy-start.7
  46.7 7.0 copy-start.13
  46.7 7.2 %copy-start.14 = (s32[32]{0:T(128)S(1)}, s32[32]{0:T(128)}, u32[]{:S(2)}) copy-start(s32[32]{0:T(128)} %param.21) | copy-start | bytes 388
  46.7 77.9 %all-to-all-start = ((bf16[256,8,512]{2,0,1:T(8,128)(2,1)}), bf16[256,8,512]{2,0,1:T(8,128)(2,1)}, u32[]{:S(2)}, u32[]{:S(2)}) async-start(bf16[256,8,512]{2,0,1:T(8,128)(2,1)} %bitcast.97), calls=%async_computation | async-start | bytes 4194304 | tf_op jit(solution)/shard_map/all_to_all | solution.py:105
  52.3 357.6 %reduce-scatter.3.cloned.1.call-start = ((), (), s32[]{:S(2)}) async-start(), calls=%async_computation.5 | async-start | bytes 16515072 | tf_op jit(solution)/shard_map/reduce_scatter | solution.py:36
  53.8 363.6 %copy-start.11 = (s32[256]{0:T(256)}, s32[256]{0:T(256)S(1)}, u32[]{:S(2)}) copy-start(s32[256]{0:T(256)S(1)} %select_reduce_fusion.1) | copy-start | bytes 3076
  136.7 3.1 copy-start.4
  136.7 3.1 copy-start.16
  139.8 1.3 copy-start.17
  173.1 1.4 copy-start.5
  173.1 409.3 %all-gather.9.cloned.1.call-start = ((), (), s32[]{:S(2)}) async-start(), calls=%async_computation.7 | async-start | bytes 11796480 | tf_op jit(solution)/shard_map/all_gather | solution.py:40
  174.5 243.0 %copy-start.9 = (s32[1024]{0:T(1024)}, s32[1024]{0:T(1024)S(1)}, u32[]{:S(2)}) copy-start(s32[1024]{0:T(1024)S(1)} %get-tuple-element.19) | copy-start | bytes 12292
  229.1 184.7 %copy-start.15 = (bf16[1024,512]{1,0:T(8,128)(2,1)S(1)}, bf16[1024,512]{1,0:T(8,128)(2,1)}, u32[]{:S(2)}) copy-start(bf16[1024,512]{1,0:T(8,128)(2,1)} %param.31) | copy-start | bytes 3145732
  411.9 1.8 copy-start.3
  425.4 0.7 copy-start.10
  425.4 0.7 copy-start.12
  425.5 0.7 copy-start.18
  432.4 157.7 %copy-start.6 = (bf16[512,512]{1,0:T(8,128)(2,1)S(1)}, bf16[512,512]{1,0:T(8,128)(2,1)}, u32[]{:S(2)}) copy-start(bf16[512,512]{1,0:T(8,128)(2,1)} %param.29) | copy-start | bytes 1572868
  432.4 256.8 %reduce-scatter.5.cloned.1.call-start = ((), (), s32[]{:S(2)}) async-start(), calls=%async_computation.6 | async-start | bytes 2621440 | tf_op jit(solution)/shard_map/reduce_scatter | solution.py:158
  654.3 36.9 %copy-start.1 = (bf16[512,2048]{1,0:T(8,128)(2,1)S(1)}, bf16[512,2048]{1,0:T(8,128)(2,1)}, u32[]{:S(2)}) copy-start(bf16[512,2048]{1,0:T(8,128)(2,1)} %param.34) | copy-start | bytes 6291460
  658.5 30.6 %copy-start.2 = (bf16[32,8,1024]{2,1,0:T(8,128)(2,1)S(1)}, bf16[32,8,1024]{2,1,0:T(8,128)(2,1)}, u32[]{:S(2)}) copy-start(bf16[32,8,1024]{2,1,0:T(8,128)(2,1)} %param.20) | copy-start | bytes 1572868
  658.5 30.6 %copy-start.8 = (f32[1024]{0:T(1024)S(1)}, f32[1024]{0:T(1024)}, u32[]{:S(2)}) copy-start(f32[1024]{0:T(1024)} %param.39) | copy-start | bytes 12292
Sparse Core Ops, SparseCore 0:
  19.2 24.3 all-gather.6
  173.3 236.6 reduce-scatter.2
  432.5 149.9 all-gather.8
  658.7 30.4 reduce-scatter.4

commit v2 on v1

--- a/solution.py
+++ b/solution.py
@@ -1,6 +1,10 @@
+import functools
+
 import jax
 import jax.numpy as jnp
 from jax import lax
+from jax.experimental import pallas as pl
+from jax.experimental.pallas import tpu as pltpu
 from jax.sharding import PartitionSpec as P
 
 HS = 256
@@ -32,12 +36,487 @@
     return jnp.where(turned[None, :], block * jnp.cos(angle) + other * jnp.sin(angle), block)
 
 
-def scatter_sum(part):
-    return lax.psum_scatter(part, "req", scatter_dimension=0, tiled=False)
-
-
-def gather_rows(act):
-    return lax.all_gather(act, "req", axis=0, tiled=False)
+MESH = pl.DeviceIdType.MESH
+VM = pl.BlockSpec(memory_space=pltpu.VMEM)
+TILE = 512
+
+
+def params(collective_id, mib):
+    return pltpu.CompilerParams(
+        collective_id=collective_id, has_side_effects=True, vmem_limit_bytes=mib << 20
+    )
+
+
+def signal(barrier, target):
+    pl.semaphore_signal(barrier, inc=1, device_id=target, device_id_type=MESH)
+
+
+def ring_place(index, n):
+    turn, height = index % 2, index // 2
+    return height + turn * (n - 1 - 2 * height)
+
+
+def ring_index(place, n):
+    turn = place // (n // 2)
+    return 2 * (place + turn * (n - 1 - 2 * place)) + turn
+
+
+def ring_ids(n):
+    place = ring_place(lax.axis_index("req"), n)
+    lane = lax.axis_index("mlp")
+    right = (ring_index((place + 1) % n, n), lane)
+    left = (ring_index((place + n - 1) % n, n), lane)
+    return place, (right, left)
+
+
+def ring_barrier(targets):
+    barrier = pltpu.get_barrier_semaphore()
+    for target in targets:
+        signal(barrier, target)
+    pl.semaphore_wait(barrier, 2)
+
+
+def reduce_kernel(n, x_ref, w_ref, extra_ref, sum_ref, esum_ref, first, got, egot, sends, recvs):
+    half = n // 2
+    tiles = w_ref.shape[0]
+    rows = x_ref.shape[1]
+    mid = rows // 2
+    place, targets = ring_ids(n)
+    ring_barrier(targets)
+    spans = (pl.ds(0, mid), pl.ds(mid, mid))
+
+    def owner(side, step):
+        away = half - step if side == 0 else n - half + step
+        return ring_index((place + away) % n, n)
+
+    def own(index, t):
+        return mm(x_ref[index], w_ref[t])
+
+    def move(side, step, t, extra=False):
+        slot = tiles if extra else t
+        buffer = egot if extra else got
+        if step == 0:
+            src = buffer.at[2 * half, spans[side]] if extra else first.at[t, spans[side]]
+            at = (side * half, spans[side])
+        else:
+            at = (side * half + step,)
+            src = buffer.at[side * half + step - 1] if extra else got.at[side * half + step - 1, t]
+        if not extra:
+            at = (at[0], t) + at[1:]
+        return pltpu.make_async_remote_copy(
+            src_ref=src,
+            dst_ref=buffer.at[at],
+            send_sem=sends.at[side * half + step, slot],
+            recv_sem=recvs.at[side * half + step, slot],
+            device_id=targets[side],
+            device_id_type=MESH,
+        )
+
+    egot[2 * half] = extra_ref[owner(0, 0)]
+    for side in (0, 1):
+        move(side, 0, 0, True).start()
+
+    @pl.loop(0, tiles)
+    def _(t):
+        first[t] = own(owner(0, 0), t).astype(bf16)
+        for side in (0, 1):
+            move(side, 0, t).start()
+
+    for step in range(1, half):
+        for side in (0, 1):
+            slot = side * half + step - 1
+            mine = extra_ref[owner(side, step)]
+            move(side, step - 1, 0, True).wait_recv()
+            if step == 1:
+                egot[slot, spans[side]] += mine[side * mid : side * mid + mid]
+                egot[slot, spans[1 - side]] = mine[(1 - side) * mid : (1 - side) * mid + mid]
+            else:
+                egot[slot] += mine
+            move(side, step, 0, True).start()
+
+        @pl.loop(0, tiles)
+        def _(t):
+            for side in (0, 1):
+                slot = side * half + step - 1
+                mine = own(owner(side, step), t)
+                move(side, step - 1, t).wait_recv()
+                if step == 1:
+                    a = mine[side * mid : side * mid + mid]
+                    b = mine[(1 - side) * mid : (1 - side) * mid + mid]
+                    here = got[slot, t, spans[side]].astype(f32)
+                    got[slot, t, spans[side]] = (here + a).astype(bf16)
+                    got[slot, t, spans[1 - side]] = b.astype(bf16)
+                else:
+                    got[slot, t] = (got[slot, t].astype(f32) + mine).astype(bf16)
+                move(side, step, t).start()
+
+    for side in (0, 1):
+        move(side, half - 1, 0, True).wait_recv()
+    me = lax.axis_index("req")
+    esum_ref[...] = extra_ref[me] + egot[half - 1] + egot[2 * half - 1]
+
+    @pl.loop(0, tiles)
+    def _(t):
+        mine = own(me, t)
+        for side in (0, 1):
+            move(side, half - 1, t).wait_recv()
+        sum_ref[t] = mine + got[half - 1, t].astype(f32) + got[2 * half - 1, t].astype(f32)
+
+    for step in range(half):
+        for side in (0, 1):
+            move(side, step, 0, True).wait_send()
+
+        @pl.loop(0, tiles)
+        def _(t):
+            for side in (0, 1):
+                move(side, step, t).wait_send()
+
+
+def reduce_rows(x, w, extra):
+    n, rows, _ = x.shape
+    tiles = w.shape[0]
+    pad = extra.shape[2]
+    return pl.pallas_call(
+        functools.partial(reduce_kernel, n),
+        out_shape=(
+            jax.ShapeDtypeStruct((tiles, rows, TILE), f32),
+            jax.ShapeDtypeStruct((rows, pad), bf16),
+        ),
+        in_specs=[VM] * 3,
+        out_specs=(VM, VM),
+        scratch_shapes=[
+            pltpu.VMEM((tiles, rows, TILE), bf16),
+            pltpu.VMEM((n, tiles, rows, TILE), bf16),
+            pltpu.VMEM((n + 1, rows, pad), bf16),
+            pltpu.SemaphoreType.DMA((n, tiles + 1)),
+            pltpu.SemaphoreType.DMA((n, tiles + 1)),
+        ],
+        compiler_params=params(1, 48),
+        name="reduce_rows",
+    )(x, w, extra)
+
+
+def gather_kernel(n, act_ref, w_ref, out_ref, got, total, sends, recvs):
+    half = n // 2
+    tiles = w_ref.shape[0]
+    rows = act_ref.shape[1]
+    mid = rows // 2
+    place, targets = ring_ids(n)
+    ring_barrier(targets)
+    spans = (pl.ds(0, mid), pl.ds(mid, mid))
+
+    def move(side, step, t):
+        src = act_ref.at[t] if step == 0 else got.at[side * half + step - 1, t]
+        dst = got.at[side * half + step, t]
+        if step == half - 1:
+            dst = got.at[half - 1, t, spans[side]]
+            src = src.at[spans[side]]
+        return pltpu.make_async_remote_copy(
+            src_ref=src,
+            dst_ref=dst,
+            send_sem=sends.at[side * half + step, t],
+            recv_sem=recvs.at[side * half + step, t],
+            device_id=targets[side],
+            device_id_type=MESH,
+        )
+
+    @pl.loop(0, tiles)
+    def _(t):
+        for side in (0, 1):
+            move(side, 0, t).start()
+
+    total[...] = jnp.zeros_like(total)
+
+    @pl.loop(0, tiles)
+    def _(t):
+        total[0] += mm(act_ref[t], w_ref[t])
+
+    out_ref[lax.axis_index("req")] = total[0].astype(bf16)
+
+    for step in range(1, half):
+        total[...] = jnp.zeros_like(total)
+
+        @pl.loop(0, tiles)
+        def _(t):
+            for side in (0, 1):
+                move(side, step - 1, t).wait_recv()
+                move(side, step, t).start()
+            for side in (0, 1):
+                total[side] += mm(got[side * half + step - 1, t], w_ref[t])
+
+        for side in (0, 1):
+            away = n - step if side == 0 else step
+            out_ref[ring_index((place + away) % n, n)] = total[side].astype(bf16)
+
+    total[...] = jnp.zeros_like(total)
+
+    @pl.loop(0, tiles)
+    def _(t):
+        for side in (0, 1):
+            move(side, half - 1, t).wait_recv()
+        total[0] += mm(got[half - 1, t], w_ref[t])
+
+    out_ref[ring_index((place + half) % n, n)] = total[0].astype(bf16)
+
+    for step in range(half):
+
+        @pl.loop(0, tiles)
+        def _(t):
+            for side in (0, 1):
+                move(side, step, t).wait_send()
+
+
+def gather_multiply(act, w, n):
+    tiles, rows, _ = act.shape
+    return pl.pallas_call(
+        functools.partial(gather_kernel, n),
+        out_shape=jax.ShapeDtypeStruct((n, rows, w.shape[2]), bf16),
+        in_specs=[VM] * 2,
+        out_specs=VM,
+        scratch_shapes=[
+            pltpu.VMEM((n, tiles, rows, TILE), bf16),
+            pltpu.VMEM((2, rows, w.shape[2]), f32),
+            pltpu.SemaphoreType.DMA((n, tiles)),
+            pltpu.SemaphoreType.DMA((n, tiles)),
+        ],
+        compiler_params=params(2, 48),
+        name="gather_multiply",
+    )(act, w)
+
+
+def exchange_barrier(n, lanes):
+    me, lane = lax.axis_index("req"), lax.axis_index("mlp")
+    per = n // lanes
+    alone = jnp.where(me // per == lane, 1, 0)
+    barrier = pltpu.get_barrier_semaphore()
+    for k in range(1, lanes):
+        signal(barrier, (me, (lane + k) % lanes))
+
+    @pl.loop(0, n)
+    def _(i):
+        there, t = lane * per + i // lanes, i % lanes
+
+        @pl.when((there != me) | (t != lane))
+        def _():
+            signal(barrier, (there, t))
+
+        @pl.when((i != me) | (me // per != lane))
+        def _():
+            signal(barrier, (i, me // per))
+
+    pl.semaphore_wait(barrier, lanes - 1 + 2 * (n - alone))
+
+
+def spread_kernel(n, lanes, x_ref, pick_ref, all_ref, picks_ref, sends, recvs, msends, mrecvs, ps, pr):
+    me, lane = lax.axis_index("req"), lax.axis_index("mlp")
+    per = n // lanes
+    exchange_barrier(n, lanes)
+
+    def out_move(j, t, source):
+        return pltpu.make_async_remote_copy(
+            src_ref=x_ref.at[j, t],
+            dst_ref=all_ref.at[source, t],
+            send_sem=sends.at[j, t],
+            recv_sem=recvs.at[source],
+            device_id=(lane * per + j, t),
+            device_id_type=MESH,
+        )
+
+    def in_move(source):
+        return pltpu.make_async_remote_copy(
+            src_ref=x_ref.at[0, lane],
+            dst_ref=all_ref.at[source, lane],
+            send_sem=sends.at[0, lane],
+            recv_sem=recvs.at[source],
+            device_id=(source, me // per),
+            device_id_type=MESH,
+        )
+
+    def fan(k, source, t):
+        return pltpu.make_async_remote_copy(
+            src_ref=all_ref.at[source, t],
+            dst_ref=all_ref.at[source, t],
+            send_sem=msends.at[k, source],
+            recv_sem=mrecvs.at[t, source],
+            device_id=(me, (lane + k) % lanes),
+            device_id_type=MESH,
+        )
+
+    def share(k, t):
+        return pltpu.make_async_remote_copy(
+            src_ref=pick_ref,
+            dst_ref=picks_ref.at[t],
+            send_sem=ps.at[k],
+            recv_sem=pr.at[t],
+            device_id=(me, (lane + k) % lanes),
+            device_id_type=MESH,
+        )
+
+    @pl.loop(0, n)
+    def _(i):
+        j, t = i // lanes, i % lanes
+        self = (lane * per + j == me) & (t == lane)
+
+        @pl.when(jnp.logical_not(self))
+        def _():
+            out_move(j, t, me).start()
+
+        @pl.when(self)
+        def _():
+            all_ref[me, lane] = x_ref[j, t]
+
+    for k in range(1, lanes):
+        share(k, lane).start()
+    picks_ref[lane] = pick_ref[...]
+
+    @pl.loop(0, n)
+    def _(i):
+        source = (me + i) % n
+
+        @pl.when((source != me) | (me // per != lane))
+        def _():
+            in_move(source).wait_recv()
+
+        for k in range(1, lanes):
+            fan(k, source, lane).start()
+
+    @pl.loop(0, n)
+    def _(source):
+        for k in range(1, lanes):
+            fan(k, source, (lane + k) % lanes).wait_recv()
+
+    for k in range(1, lanes):
+        share(k, (lane + k) % lanes).wait_recv()
+        share(k, lane).wait_send()
+
+    @pl.loop(0, n)
+    def _(i):
+        j, t = i // lanes, i % lanes
+
+        @pl.when((lane * per + j != me) | (t != lane))
+        def _():
+            out_move(j, t, me).wait_send()
+
+        for k in range(1, lanes):
+            fan(k, i, lane).wait_send()
+
+
+def spread_rows(x, picked, n, lanes):
+    _, _, part, chunk = x.shape
+    return pl.pallas_call(
+        functools.partial(spread_kernel, n, lanes),
+        out_shape=(
+            jax.ShapeDtypeStruct((n, lanes, part, chunk), bf16),
+            jax.ShapeDtypeStruct((lanes,) + picked.shape, bf16),
+        ),
+        in_specs=[VM] * 2,
+        out_specs=(VM, VM),
+        scratch_shapes=[
+            pltpu.SemaphoreType.DMA((n // lanes, lanes)),
+            pltpu.SemaphoreType.DMA((n,)),
+            pltpu.SemaphoreType.DMA((lanes, n)),
+            pltpu.SemaphoreType.DMA((lanes, n)),
+            pltpu.SemaphoreType.DMA((lanes,)),
+            pltpu.SemaphoreType.DMA((lanes,)),
+        ],
+        compiler_params=params(3, 24),
+        name="spread_rows",
+    )(x, picked)
+
+
+def collect_kernel(n, lanes, y_ref, out_ref, part, ready, msends, mrecvs, sends, recvs):
+    me, lane = lax.axis_index("req"), lax.axis_index("mlp")
+    per = n // lanes
+    exchange_barrier(n, lanes)
+
+    def cross(k, d):
+        return pltpu.make_async_remote_copy(
+            src_ref=y_ref.at[d, (lane + k) % lanes],
+            dst_ref=part.at[k - 1, d],
+            send_sem=msends.at[k - 1, d],
+            recv_sem=mrecvs.at[k - 1, d],
+            device_id=(me, (lane + k) % lanes),
+            device_id_type=MESH,
+        )
+
+    def home(d):
+        return pltpu.make_async_remote_copy(
+            src_ref=ready.at[d],
+            dst_ref=out_ref.at[me % per, lane],
+            send_sem=sends.at[d],
+            recv_sem=recvs.at[me % per, lane],
+            device_id=(d, me // per),
+            device_id_type=MESH,
+        )
+
+    def arrive(j, t):
+        return pltpu.make_async_remote_copy(
+            src_ref=ready.at[0],
+            dst_ref=out_ref.at[j, t],
+            send_sem=sends.at[0],
+            recv_sem=recvs.at[j, t],
+            device_id=(lane * per + j, t),
+            device_id_type=MESH,
+        )
+
+    @pl.loop(0, n)
+    def _(i):
+        for k in range(1, lanes):
+            cross(k, (me + i) % n).start()
+
+    @pl.loop(0, n)
+    def _(i):
+        d = (me + i) % n
+        total = y_ref[d, lane].astype(f32)
+        for k in range(1, lanes):
+            cross(k, d).wait_recv()
+            total += part[k - 1, d].astype(f32)
+        ready[d] = total.astype(bf16)
+        self = (d == me) & (me // per == lane)
+
+        @pl.when(jnp.logical_not(self))
+        def _():
+            home(d).start()
+
+        @pl.when(self)
+        def _():
+            out_ref[me % per, lane] = total.astype(bf16)
+
+    @pl.loop(0, n)
+    def _(i):
+        j, t = i // lanes, i % lanes
+
+        @pl.when((lane * per + j != me) | (t != lane))
+        def _():
+            arrive(j, t).wait_recv()
+
+        @pl.when((i != me) | (me // per != lane))
+        def _():
+            home(i).wait_send()
+
+        for k in range(1, lanes):
+            cross(k, i).wait_send()
+
+
+def collect_rows(y):
+    n, lanes, rows, chunk = y.shape
+    per = n // lanes
+    return pl.pallas_call(
+        functools.partial(collect_kernel, n, lanes),
+        out_shape=jax.ShapeDtypeStruct((per, lanes, rows, chunk), bf16),
+        in_specs=[VM],
+        out_specs=VM,
+        scratch_shapes=[
+            pltpu.VMEM((lanes - 1, n, rows, chunk), bf16),
+            pltpu.VMEM((n, rows, chunk), bf16),
+            pltpu.SemaphoreType.DMA((lanes - 1, n)),
+            pltpu.SemaphoreType.DMA((lanes - 1, n)),
+            pltpu.SemaphoreType.DMA((n,)),
+            pltpu.SemaphoreType.DMA((per, lanes)),
+        ],
+        compiler_params=params(4, 24),
+        name="collect_rows",
+    )(y)
 
 
 def on_device(
@@ -101,11 +580,6 @@
     bias = lax.dynamic_slice_in_dim(ln_bias, column, width_m, 0)
     normed = ((x - mean[:, None]) * scale[:, None] * gain + bias).astype(bf16)
 
-    full_rows = lax.all_gather(normed, "mlp", axis=1, tiled=True)
-    everyone = lax.all_to_all(full_rows, "req", split_axis=1, concat_axis=0, tiled=True)
-    ordered = mm(perm_low, everyone.reshape(pages, page_len * chunk)).astype(bf16)
-    ordered = ordered.reshape(groups * tok, chunk)
-
     col_adapter = jnp.arange(NAD * R) // R
     fold = (jnp.arange(NAD * R)[:, None] % R == jnp.arange(R)[None, :]).astype(bf16)
     held_mask = held_adapter[:, None] == col_adapter[None, :]
@@ -114,21 +588,37 @@
         return mm(jnp.where(held_mask, mm(normed, down), 0.0).astype(bf16), fold)
 
     picked = jnp.concatenate([pick(down_query), pick(down_value), pick(down_fc)], axis=1)
-    picked = lax.all_gather(picked.astype(bf16), ("req", "mlp"), axis=0, tiled=False)
-    picked = jnp.sum(picked.reshape(groups, lanes, tok, 3 * R).astype(f32), axis=1).astype(bf16)
-    own_perm = lax.dynamic_slice_in_dim(perm_low, me * pg_dev, pg_dev, 0)
-    chosen = mm(own_perm, picked.reshape(pages, page_len * 3 * R)).astype(bf16)
-    chosen = chosen.reshape(tok, 3 * R)
+    pad = 128
+    picked = jnp.pad(picked.astype(bf16), ((0, 0), (0, pad - 3 * R)))
+
+    per = groups // lanes
+    part = tok // lanes
+    pieces = normed.reshape(lanes, part, per, chunk).transpose(2, 0, 1, 3)
+    everyone, picks = spread_rows(pieces, picked, groups, lanes)
+    ordered = mm(perm_low, everyone.reshape(pages, page_len * chunk)).astype(bf16)
+    ordered = ordered.reshape(groups, tok, chunk)
+
+    held_chosen = jnp.sum(picks.astype(f32), axis=0).astype(bf16)
+    held_perm = lax.dynamic_slice_in_dim(perm_low, me * pg_dev, pg_dev, 1)
+    placed = mm(held_perm, held_chosen.reshape(pg_dev, page_len * pad)).astype(bf16)
+    placed = placed.reshape(groups, tok, pad)
     own_mask = adapter[:, None] == col_adapter[None, :]
 
     def lift(low, up):
         wide = mm(low, fold.T).astype(bf16)
         return mm(jnp.where(own_mask, wide, jnp.zeros((), bf16)), up)
 
-    part = jnp.concatenate(
-        [mm(ordered, w).astype(bf16) for w in (w_query, w_key, w_value, w_fc_in)], axis=1
-    )
-    base = scatter_sum(part.reshape(groups, tok, 3 * heads_w + ff)).astype(f32)
+    total = 3 * heads_w + ff
+    w_in = jnp.concatenate([w_query, w_key, w_value, w_fc_in], axis=1)
+    if groups <= 8:
+        w_tiles = w_in.reshape(chunk, total // TILE, TILE).transpose(1, 0, 2)
+        base, chosen = reduce_rows(ordered, w_tiles, placed)
+        base = base.transpose(1, 0, 2).reshape(tok, total)
+    else:
+        part_sum = mm(ordered.reshape(groups * tok, chunk), w_in).astype(bf16)
+        part_sum = part_sum.reshape(groups, tok, total)
+        base = lax.psum_scatter(part_sum, "req", scatter_dimension=0, tiled=False).astype(f32)
+        chosen = lax.psum_scatter(placed, "req", scatter_dimension=0, tiled=False)
 
     row_iota = jnp.arange(tok)
     start = jnp.sum((request_id[None, :] < request_id[:, None]).astype(jnp.int32), axis=1)
@@ -147,15 +637,20 @@
     probs = (weights / jnp.sum(weights, axis=2, keepdims=True)).astype(bf16)
     attn = jnp.einsum("hqk,khd->qhd", probs, value, preferred_element_type=f32)
     attn = attn.astype(bf16).reshape(tok, heads_w)
-    hidden = gelu_tanh(base[:, 3 * heads_w :] + lift(chosen[:, 2 * R :], up_fc) + b_fc_in)
+    hidden = gelu_tanh(base[:, 3 * heads_w :] + lift(chosen[:, 2 * R : 3 * R], up_fc) + b_fc_in)
     act = jnp.concatenate([attn, hidden.astype(bf16)], axis=1)
 
-    acts = gather_rows(act).reshape(groups * tok, heads_w + ff)
-    out = mm(acts[:, :heads_w], w_attn_out) + mm(acts[:, heads_w:], w_fc_out)
-    out = out.astype(bf16).reshape(pages, page_len * chunk)
-    out = mm(perm_low.T, out).astype(bf16).reshape(groups * tok, chunk)
-    shares = lax.all_to_all(out, "req", split_axis=0, concat_axis=1, tiled=True)
-    shares = lax.psum_scatter(shares, "mlp", scatter_dimension=1, tiled=True)
+    w_out = jnp.concatenate([w_attn_out, w_fc_out], axis=0)
+    if groups <= 8:
+        tiles = (heads_w + ff) // TILE
+        act = act.reshape(tok, tiles, TILE).transpose(1, 0, 2)
+        out = gather_multiply(act, w_out.reshape(tiles, TILE, chunk), groups)
+    else:
+        acts = lax.all_gather(act, "req", axis=0, tiled=False)
+        out = mm(acts.reshape(groups * tok, heads_w + ff), w_out).astype(bf16)
+    out = mm(perm_low.T, out.reshape(pages, page_len * chunk)).astype(bf16)
+    shares = collect_rows(out.reshape(groups, lanes, part, chunk))
+    shares = shares.transpose(1, 2, 0, 3).reshape(tok, width_m)
     result = (x + shares.astype(f32) + b_fc_out).astype(bf16)
     return result.reshape(pg_dev, page_len, width_m)
 

time: 699 us -> 483 us (0.69)
  waiting for transfers between devices: 386 us -> 0 us
  Pallas kernels: 0 us -> 338 us
  blocking collectives: 173 us -> 44 us
  matrix products: 45 us -> 22.8 us
  between operations: 14.2 us -> 1.08 us
    pallas_call x0 -> x4, Pallas kernels: none -> 338 us  [the longest x1 160 us: reduce_rows(): pl.pallas_call(functools.partial(reduce_kernel, n), out_shape=(jax.ShapeD...]
    reduce_scatter x2 -> x0, waiting for transfers between devices: 211 us -> none  [the longest x1 181 us: scatter_sum(): return lax.psum_scatter(part, 'req', scatter_dimension=0, tiled=False)]
    all_gather x2 -> x0, waiting for transfers between devices: 174 us -> none  [the longest x1 150 us: gather_rows(): return lax.all_gather(act, 'req', axis=0, tiled=False)]
    all_to_all x1 -> x0, blocking collectives: 51.3 us -> none  [on_device(): shares = lax.all_to_all(out, 'req', split_axis=0, concat_axis=1, tiled=True)]
    all_gather x1 -> x0, blocking collectives: 44.9 us -> none  [on_device(): lax.all_gather(picked.astype(bf16), ('req', 'mlp'), axis=0, tiled=False)]
    unnamed x1, blocking collectives: 70.2 us -> 38.8 us
    dot_general x15 -> x9, matrix products: 44.4 us -> 22.2 us  [mm(): return jnp.dot(a, b, preferred_element_type=f32)]
    unnamed x42 -> x36, local copies, waits for them, and re-layouts: 2.52 us -> 15.6 us
  transfers between devices with their start and end apart: 5 -> 0, of which waited for: 4 -> 0; matrix products, arithmetic and copies ran while one was open for 2% -> 0% of each run, Pallas kernels for 0% -> 0%
where the time goes in v2:
time: 483 us; the launch traced here: 482 us
  Pallas kernels  338 us (70%)
  local copies, waits for them, and re-layouts  57 us (12%)
  blocking collectives  44 us (9%)
  matrix products  22.8 us (5%)
  other arithmetic  18.5 us (4%)
    pallas_call x1, Pallas kernels, reduce_rows(): pl.pallas_call(functools.partial(reduce_kernel, n), out_shape=(jax.ShapeD...  160 us
    pallas_call x1, Pallas kernels, gather_multiply(): pl.pallas_call(functools.partial(gather_kernel, n), out_shape=jax.ShapeDt...  102 us
    pallas_call x1, Pallas kernels, spread_rows(): pl.pallas_call(functools.partial(spread_kernel, n, lanes), out_shape=(jax...  39.4 us
    unnamed x1, blocking collectives  38.8 us
    pallas_call x1, Pallas kernels, collect_rows(): pl.pallas_call(functools.partial(collect_kernel, n, lanes), out_shape=jax...  36.3 us
    dot_general x9, matrix products, mm(): return jnp.dot(a, b, preferred_element_type=f32)  22.2 us
    unnamed x36, local copies, waits for them, and re-layouts  15.6 us

profile of v2, /device:TPU:0, one launch (start us, length us, event | category | flops | bytes accessed | tf_op | source)
XLA Modules:
  0.0 481.6 jit_solution(12143778417851202202)
XLA Ops:
  4.5 38.8 %all-reduce.1 = s32[2304]{0:T(1024)S(1)} all-reduce(s32[2304]{0:T(1024)S(1)} %add_dynamic-update-slice_fusion), channel_id=2, replica_groups=mesh['req'=8,'mlp'=4] {'req'}, use_global_device_ids=true, to_apply=%add.1 | all-reduce | flops 2304 | bytes 18432
  47.5 5.2 %all-gather.2 = f32[4,2,256]{2,1,0:T(2,128)S(1)} all-gather(f32[1,2,256]{2,1,0:T(2,128)S(1)} %maximum_bitcast_fusion), channel_id=3, replica_groups=mesh['req'=8,'mlp'=4] {'mlp'}, dimensions={0}, use_global_device_ids=true | all-gather | bytes 10240 | tf_op jit(solution)/shard_map/all_gather | solution.py:574
  54.1 2.1 fusion.21
  56.2 2.6 fusion.22
  58.7 2.6 fusion.23
  63.1 39.4 %spread_rows.1 = (bf16[8,4,64,512]{3,2,1,0:T(8,128)(2,1)S(1)}, bf16[4,256,128]{2,1,0:T(8,128)(2,1)S(1)}) custom-call(bf16[2,4,64,512]{3,2,1,0:T(8,128)(2,1)S(1)} %fusion.32.x_ref, bf16[256,128]{1,0:T(8,128)(2,1)S(1)} %pad.4.pick_ref), custom_call_target="tpu_custom_call" | custom-call | tf_op jit(solution)/shard_map/spread_rows/pallas_call | solution.py:406
  102.5 2.4 reshape.291
  104.9 3.6 convolution_convert_fusion.1
  108.5 2.9 reshape.292.x_ref
  112.1 3.9 copy.89
  117.3 2.1 copy.87
  119.3 2.0 copy.88
  121.4 3.3 pad_maximum_fusion
  124.7 6.3 %copy.90 = bf16[512,7,512]{2,0,1:T(8,128)(2,1)} copy(bf16[512,7,512]{0,2,1:T(8,128)(2,1)} %bitcast.76) | data formatting | bytes 7340032 | tf_op jit(solution)/shard_map/reshape | solution.py:614
  130.9 160.5 %reduce_rows.1 = (f32[7,256,512]{2,1,0:T(8,128)}, bf16[256,128]{1,0:T(8,128)(2,1)S(1)}) custom-call(bf16[8,256,512]{2,1,0:T(8,128)(2,1)S(1)} %reshape.292.x_ref, bf16[7,512,512]{2,1,0:T(8,128)(2,1)} %bitcast.77, bf16[8,256,128]{2,1,0:T(8,128)(2,1)S(1)} %reshape.295.extra_ref), custom_call_target="tpu_custom_call" | custom-call | tf_op jit(solution)/shard_map/reduce_rows/pallas_call | solution.py:179
  291.4 4.6 copy.91
  296.0 2.4 fusion.124
  300.5 2.1 fusion.126
  305.2 3.5 fusion.37
  311.5 1.7 slice.100
  313.2 1.9 copy.119
  315.1 6.0 %fusion.6 = bf16[256,2048]{1,0:T(8,128)(2,1)} fusion(f32[256,2048]{1,0:T(8,128)} %copy.119, bf16[1024,2048]{1,0:T(8,128)(2,1)} %param.37, f32[2048]{0:T(1024)S(1)} %copy-done.10, s32[1024]{0:T(1024)S(1)} %get-tuple-element.30, s32[256]{0:T(256)S(1)} %select_reduce_fusion.1, s32[1024]{0:T(1024)S(1)} %get-tuple-element.29, ...), kind=kOutput, calls=%fused_computation.12 | convolution fusion | flops 1088700416 | bytes 7422976 | tf_op jit(solution)/shard_map/dot_general | solution.py:21
  322.4 1.5 copy.105
  323.8 1.7 copy.106
  327.0 102.0 %gather_multiply.1 = bf16[8,256,512]{2,1,0:T(8,128)(2,1)S(1)} custom-call(bf16[5,256,512]{2,1,0:T(8,128)(2,1)S(1)} %bitcast.71, bf16[5,512,512]{2,1,0:T(8,128)(2,1)S(1)} %bitcast.70), custom_call_target="tpu_custom_call" | custom-call | tf_op jit(solution)/shard_map/gather_multiply/pallas_call | solution.py:271
  429.1 2.4 reshape.303
  431.5 3.6 convolution_convert_fusion
  435.1 2.9 reshape.304.y_ref
  438.0 36.3 %collect_rows.1 = bf16[2,4,64,512]{3,2,1,0:T(8,128)(2,1)S(1)} custom-call(bf16[8,4,64,512]{3,2,1,0:T(8,128)(2,1)S(1)} %reshape.304.y_ref), custom_call_target="tpu_custom_call" | custom-call | tf_op jit(solution)/shard_map/collect_rows/pallas_call | solution.py:504
  474.5 1.8 copy.107
  476.3 3.2 reshape.307
  479.4 2.2 add_convert_fusion
  (92 shorter events, 23.2 us)
Async XLA Ops:
  0.0 54.1 %copy-start = (bf16[1024,1024]{1,0:T(8,128)(2,1)S(1)}, bf16[1024,1024]{1,0:T(8,128)(2,1)}, u32[]{:S(2)}) copy-start(bf16[1024,1024]{1,0:T(8,128)(2,1)} %param.30) | copy-start | bytes 6291460
  54.1 2.1 copy-start.2
  296.0 2.6 copy-start.8
  300.5 4.6 copy-start.6
  308.7 1.0 copy-start.5
  308.8 1.4 copy-start.9
  313.2 1.9 copy-start.10
  323.8 2.0 copy-start.4
  474.4 5.0 %copy-start.3 = (bf16[32,8,1024]{2,1,0:T(8,128)(2,1)S(1)}, bf16[32,8,1024]{2,1,0:T(8,128)(2,1)}, u32[]{:S(2)}) copy-start(bf16[32,8,1024]{2,1,0:T(8,128)(2,1)} %param.20) | copy-start | bytes 1572868
  474.4 5.0 %copy-start.7 = (f32[1024]{0:T(1024)S(1)}, f32[1024]{0:T(1024)}, u32[]{:S(2)}) copy-start(f32[1024]{0:T(1024)} %param.39) | copy-start | bytes 12292
  474.4 7.2 %copy-start.1 = (bf16[1024,1024]{1,0:T(8,128)(2,1)S(1)}, bf16[1024,1024]{1,0:T(8,128)(2,1)}, u32[]{:S(2)}) copy-start(bf16[1024,1024]{1,0:T(8,128)(2,1)} %param.30) | copy-start | bytes 6291460

commit v3 on v2

--- a/solution.py
+++ b/solution.py
@@ -38,6 +38,7 @@
 
 MESH = pl.DeviceIdType.MESH
 VM = pl.BlockSpec(memory_space=pltpu.VMEM)
+ANY = pl.BlockSpec(memory_space=pl.ANY)
 TILE = 512
 
 
@@ -76,9 +77,90 @@
     pl.semaphore_wait(barrier, 2)
 
 
-def reduce_kernel(n, x_ref, w_ref, extra_ref, sum_ref, esum_ref, first, got, egot, sends, recvs):
+def greet_kernel(n, lanes, int_ref, stat_ref, ints_ref, stats_ref, isend, irecv, ssend, srecv):
+    me, lane = lax.axis_index("req"), lax.axis_index("mlp")
+    barrier = pltpu.get_barrier_semaphore()
+
+    @pl.loop(1, n)
+    def _(k):
+        signal(barrier, ((me + k) % n, lane))
+
+    for k in range(1, lanes):
+        signal(barrier, (me, (lane + k) % lanes))
+    pl.semaphore_wait(barrier, n + lanes - 2)
+
+    def move(src, dst, send, recv, k, slot, target):
+        return pltpu.make_async_remote_copy(
+            src_ref=src,
+            dst_ref=dst.at[slot],
+            send_sem=send.at[k],
+            recv_sem=recv.at[slot],
+            device_id=target,
+            device_id_type=MESH,
+        )
+
+    def along_req(k, slot):
+        return move(int_ref, ints_ref, isend, irecv, k, slot, ((me + k) % n, lane))
+
+    def along_mlp(k, slot):
+        return move(stat_ref, stats_ref, ssend, srecv, k, slot, (me, (lane + k) % lanes))
+
+    for k in range(1, lanes):
+        along_mlp(k, lane).start()
+
+    @pl.loop(1, n)
+    def _(k):
+        along_req(k, me).start()
+
+    ints_ref[me] = int_ref[...]
+    stats_ref[lane] = stat_ref[...]
+    for k in range(1, lanes):
+        along_mlp(k, (lane + k) % lanes).wait_recv()
+        along_mlp(k, lane).wait_send()
+
+    @pl.loop(1, n)
+    def _(k):
+        along_req(k, (me + k) % n).wait_recv()
+        along_req(k, me).wait_send()
+
+
+def greet(ints, stats, n, lanes):
+    return pl.pallas_call(
+        functools.partial(greet_kernel, n, lanes),
+        out_shape=(
+            jax.ShapeDtypeStruct((n,) + ints.shape, jnp.int32),
+            jax.ShapeDtypeStruct((lanes,) + stats.shape, f32),
+        ),
+        in_specs=[VM] * 2,
+        out_specs=(VM, VM),
+        scratch_shapes=[
+            pltpu.SemaphoreType.DMA((n,)),
+            pltpu.SemaphoreType.DMA((n,)),
+            pltpu.SemaphoreType.DMA((lanes,)),
+            pltpu.SemaphoreType.DMA((lanes,)),
+        ],
+        compiler_params=params(5, 16),
+        name="greet",
+    )(ints, stats)
+
+
+def columns(t):
+    return pl.ds(pl.multiple_of(t * TILE, TILE), TILE)
+
+
+def reduce_kernel(
+    n, x_ref, wq_ref, wk_ref, wv_ref, wf_ref, extra_ref, sum_ref, esum_ref,
+    w_ref, first, got, egot, sends, recvs, loads,
+):
     half = n // 2
     tiles = w_ref.shape[0]
+    pieces = []
+    for ref in (wq_ref, wk_ref, wv_ref, wf_ref):
+        for c in range(ref.shape[1] // TILE):
+            t = len(pieces)
+            src = ref.at[:, pl.ds(c * TILE, TILE)]
+            pieces.append(pltpu.make_async_copy(src, w_ref.at[t], loads.at[t]))
+            pieces[-1].start()
     rows = x_ref.shape[1]
     mid = rows // 2
     place, targets = ring_ids(n)
@@ -115,6 +197,8 @@
     egot[2 * half] = extra_ref[owner(0, 0)]
     for side in (0, 1):
         move(side, 0, 0, True).start()
+    for piece in pieces:
+        piece.wait()
 
     @pl.loop(0, tiles)
     def _(t):
@@ -160,7 +244,7 @@
         mine = own(me, t)
         for side in (0, 1):
             move(side, half - 1, t).wait_recv()
-        sum_ref[t] = mine + got[half - 1, t].astype(f32) + got[2 * half - 1, t].astype(f32)
+        sum_ref[:, columns(t)] = mine + got[half - 1, t].astype(f32) + got[2 * half - 1, t].astype(f32)
 
     for step in range(half):
         for side in (0, 1):
@@ -172,41 +256,50 @@
                 move(side, step, t).wait_send()
 
 
-def reduce_rows(x, w, extra):
-    n, rows, _ = x.shape
-    tiles = w.shape[0]
+def reduce_rows(x, weights, extra):
+    n, rows, depth = x.shape
+    tiles = sum(w.shape[1] for w in weights) // TILE
     pad = extra.shape[2]
     return pl.pallas_call(
         functools.partial(reduce_kernel, n),
         out_shape=(
-            jax.ShapeDtypeStruct((tiles, rows, TILE), f32),
+            jax.ShapeDtypeStruct((rows, tiles * TILE), f32),
             jax.ShapeDtypeStruct((rows, pad), bf16),
         ),
-        in_specs=[VM] * 3,
+        in_specs=[VM] + [ANY] * 4 + [VM],
         out_specs=(VM, VM),
         scratch_shapes=[
+            pltpu.VMEM((tiles, depth, TILE), bf16),
             pltpu.VMEM((tiles, rows, TILE), bf16),
             pltpu.VMEM((n, tiles, rows, TILE), bf16),
             pltpu.VMEM((n + 1, rows, pad), bf16),
             pltpu.SemaphoreType.DMA((n, tiles + 1)),
             pltpu.SemaphoreType.DMA((n, tiles + 1)),
+            pltpu.SemaphoreType.DMA((tiles,)),
         ],
         compiler_params=params(1, 48),
         name="reduce_rows",
-    )(x, w, extra)
-
-
-def gather_kernel(n, act_ref, w_ref, out_ref, got, total, sends, recvs):
+    )(x, *weights, extra)
+
+
+def gather_kernel(n, act_ref, wa_ref, wf_ref, out_ref, w_ref, got, total, sends, recvs, loads):
     half = n // 2
     tiles = w_ref.shape[0]
-    rows = act_ref.shape[1]
+    rows = act_ref.shape[0]
+    pieces = []
+    for ref in (wa_ref, wf_ref):
+        for c in range(ref.shape[0] // TILE):
+            t = len(pieces)
+            src = ref.at[pl.ds(c * TILE, TILE)]
+            pieces.append(pltpu.make_async_copy(src, w_ref.at[t], loads.at[t]))
+            pieces[-1].start()
     mid = rows // 2
     place, targets = ring_ids(n)
     ring_barrier(targets)
     spans = (pl.ds(0, mid), pl.ds(mid, mid))
 
     def move(side, step, t):
-        src = act_ref.at[t] if step == 0 else got.at[side * half + step - 1, t]
+        src = act_ref.at[:, columns(t)] if step == 0 else got.at[side * half + step - 1, t]
         dst = got.at[side * half + step, t]
         if step == half - 1:
             dst = got.at[half - 1, t, spans[side]]
@@ -226,10 +319,12 @@
             move(side, 0, t).start()
 
     total[...] = jnp.zeros_like(total)
+    for piece in pieces:
+        piece.wait()
 
     @pl.loop(0, tiles)
     def _(t):
-        total[0] += mm(act_ref[t], w_ref[t])
+        total[0] += mm(act_ref[:, columns(t)], w_ref[t])
 
     out_ref[lax.axis_index("req")] = total[0].astype(bf16)
 
@@ -266,22 +361,26 @@
                 move(side, step, t).wait_send()
 
 
-def gather_multiply(act, w, n):
-    tiles, rows, _ = act.shape
+def gather_multiply(act, weights, n):
+    rows, depth = act.shape
+    tiles = depth // TILE
+    width = weights[0].shape[1]
     return pl.pallas_call(
         functools.partial(gather_kernel, n),
-        out_shape=jax.ShapeDtypeStruct((n, rows, w.shape[2]), bf16),
-        in_specs=[VM] * 2,
+        out_shape=jax.ShapeDtypeStruct((n, rows, width), bf16),
+        in_specs=[VM, ANY, ANY],
         out_specs=VM,
         scratch_shapes=[
+            pltpu.VMEM((tiles, TILE, width), bf16),
             pltpu.VMEM((n, tiles, rows, TILE), bf16),
-            pltpu.VMEM((2, rows, w.shape[2]), f32),
+            pltpu.VMEM((2, rows, width), f32),
             pltpu.SemaphoreType.DMA((n, tiles)),
             pltpu.SemaphoreType.DMA((n, tiles)),
+            pltpu.SemaphoreType.DMA((tiles,)),
         ],
         compiler_params=params(2, 48),
         name="gather_multiply",
-    )(act, w)
+    )(act, *weights)
 
 
 def exchange_barrier(n, lanes):
@@ -555,9 +654,18 @@
     local_req = request_id - me * tok
     lookup = local_req[:, None] == jnp.arange(tok)[None, :]
     adapter = jnp.sum(jnp.where(lookup, adapter_table[None, :], 0), axis=1)
-    ints = lax.all_gather(jnp.concatenate([page_owner, adapter]), "req", axis=0, tiled=False)
+    x = x_pages.reshape(tok, width_m).astype(f32)
+    local_mean = jnp.mean(x, axis=1)
+    local_m2 = jnp.sum(jnp.square(x - local_mean[:, None]), axis=1)
+    numbers = jnp.concatenate([page_owner, adapter])
+    count = pg_dev + tok
+    room = -(-count // 1024) * 1024
+    numbers = jnp.pad(numbers, (0, room - count)).reshape(room // 128, 128)
+    local = jnp.pad(jnp.stack([local_mean, local_m2]), ((0, 6), (0, 0)))
+    ints, stats = greet(numbers, local, groups, lanes)
+    ints = ints.reshape(groups, room)
     owner_all = ints[:, :pg_dev].reshape(pages)
-    adapter_all = ints[:, pg_dev:].reshape(pages, page_len)
+    adapter_all = ints[:, pg_dev:count].reshape(pages, page_len)
     iota = jnp.arange(pages)
     earlier = (owner_all[None, :] == owner_all[:, None]) & (iota[None, :] < iota[:, None])
     dest = owner_all * pg_dev + jnp.sum(earlier.astype(jnp.int32), axis=1)
@@ -568,10 +676,6 @@
         jnp.where((mine[:, None] == iota[None, :])[:, :, None], adapter_all[None, :, :], 0), axis=1
     ).reshape(tok)
 
-    x = x_pages.reshape(tok, width_m).astype(f32)
-    local_mean = jnp.mean(x, axis=1)
-    local_m2 = jnp.sum(jnp.square(x - local_mean[:, None]), axis=1)
-    stats = lax.all_gather(jnp.stack([local_mean, local_m2]), "mlp", axis=0, tiled=False)
     mean = jnp.mean(stats[:, 0], axis=0)
     m2 = jnp.sum(stats[:, 1] + width_m * jnp.square(stats[:, 0] - mean[None, :]), axis=0)
     scale = lax.rsqrt(m2 / width + EPS)
@@ -609,12 +713,10 @@
         return mm(jnp.where(own_mask, wide, jnp.zeros((), bf16)), up)
 
     total = 3 * heads_w + ff
-    w_in = jnp.concatenate([w_query, w_key, w_value, w_fc_in], axis=1)
     if groups <= 8:
-        w_tiles = w_in.reshape(chunk, total // TILE, TILE).transpose(1, 0, 2)
-        base, chosen = reduce_rows(ordered, w_tiles, placed)
-        base = base.transpose(1, 0, 2).reshape(tok, total)
+        base, chosen = reduce_rows(ordered, (w_query, w_key, w_value, w_fc_in), placed)
     else:
+        w_in = jnp.concatenate([w_query, w_key, w_value, w_fc_in], axis=1)
         part_sum = mm(ordered.reshape(groups * tok, chunk), w_in).astype(bf16)
         part_sum = part_sum.reshape(groups, tok, total)
         base = lax.psum_scatter(part_sum, "req", scatter_dimension=0, tiled=False).astype(f32)
@@ -640,12 +742,10 @@
     hidden = gelu_tanh(base[:, 3 * heads_w :] + lift(chosen[:, 2 * R : 3 * R], up_fc) + b_fc_in)
     act = jnp.concatenate([attn, hidden.astype(bf16)], axis=1)
 
-    w_out = jnp.concatenate([w_attn_out, w_fc_out], axis=0)
     if groups <= 8:
-        tiles = (heads_w + ff) // TILE
-        act = act.reshape(tok, tiles, TILE).transpose(1, 0, 2)
-        out = gather_multiply(act, w_out.reshape(tiles, TILE, chunk), groups)
+        out = gather_multiply(act, (w_attn_out, w_fc_out), groups)
     else:
+        w_out = jnp.concatenate([w_attn_out, w_fc_out], axis=0)
         acts = lax.all_gather(act, "req", axis=0, tiled=False)
         out = mm(acts.reshape(groups * tok, heads_w + ff), w_out).astype(bf16)
     out = mm(perm_low.T, out.reshape(pages, page_len * chunk)).astype(bf16)

time: 483 us -> 429 us (0.89)
  blocking collectives: 44 us -> 0 us
  local copies, waits for them, and re-layouts: 57 us -> 40.1 us
  Pallas kernels: 338 us -> 348 us
    unnamed x1 -> x0, blocking collectives: 38.8 us -> none
    pallas_call x0 -> x1, Pallas kernels: none -> 9.47 us  [greet(): pl.pallas_call(functools.partial(greet_kernel, n, lanes), out_shape=(jax....]
    reshape x2 -> x1, local copies, waits for them, and re-layouts: 8.01 us -> 0.01 us  [on_device(): numbers = jnp.pad(numbers, (0, room - count)).reshape(room // 128, 128)]
    unnamed x36 -> x31, local copies, waits for them, and re-layouts: 15.6 us -> 9.5 us
    all_gather x1 -> x0, blocking collectives: 5.17 us -> none  [on_device(): lax.all_gather(jnp.stack([local_mean, local_m2]), 'mlp', axis=0, tiled=Fa...]
where the time goes in v3:
time: 429 us; the launch traced here: 428 us
  Pallas kernels  348 us (81%)
  local copies, waits for them, and re-layouts  40.1 us (9%)
  matrix products  25.4 us (6%)
  other arithmetic  14.3 us (3%)
    pallas_call x1, Pallas kernels, reduce_rows(): pl.pallas_call(functools.partial(reduce_kernel, n), out_shape=(jax.ShapeD...  158 us
    pallas_call x1, Pallas kernels, gather_multiply(): pl.pallas_call(functools.partial(gather_kernel, n), out_shape=jax.ShapeDt...  102 us
    pallas_call x1, Pallas kernels, spread_rows(): pl.pallas_call(functools.partial(spread_kernel, n, lanes), out_shape=(jax...  41.3 us
    pallas_call x1, Pallas kernels, collect_rows(): pl.pallas_call(functools.partial(collect_kernel, n, lanes), out_shape=jax...  36.7 us
    dot_general x9, matrix products, mm(): return jnp.dot(a, b, preferred_element_type=f32)  24.8 us
    unnamed x31, local copies, waits for them, and re-layouts  9.5 us
    pallas_call x1, Pallas kernels, greet(): pl.pallas_call(functools.partial(greet_kernel, n, lanes), out_shape=(jax....  9.47 us

profile of v3, /device:TPU:0, one launch (start us, length us, event | category | flops | bytes accessed | tf_op | source)
XLA Modules:
  0.0 428.0 jit_solution(16354397176649143382)
XLA Ops:
  2.4 1.2 convert_reduce_fusion
  3.6 1.3 multiply_reduce_fusion
  5.2 9.5 %greet.1 = (s32[8,8,128]{2,1,0:T(8,128)S(1)}, f32[4,8,256]{2,1,0:T(8,128)S(1)}) custom-call(s32[8,128]{1,0:T(8,128)S(1)} %pad_bitcast_fusion.int_ref, f32[8,256]{1,0:T(8,128)S(1)} %select_maximum_fusion.stat_ref), custom_call_target="tpu_custom_call" | custom-call | tf_op jit(solution)/shard_map/greet/pallas_call | solution.py:128
  17.5 2.1 fusion.21
  19.6 2.6 fusion.22
  22.2 2.6 fusion.23
  25.1 1.9 reshape.297
  27.0 1.6 fusion.32.x_ref
  28.6 41.3 %spread_rows.1 = (bf16[8,4,64,512]{3,2,1,0:T(8,128)(2,1)S(1)}, bf16[4,256,128]{2,1,0:T(8,128)(2,1)S(1)}) custom-call(bf16[2,4,64,512]{3,2,1,0:T(8,128)(2,1)S(1)} %fusion.32.x_ref, bf16[256,128]{1,0:T(8,128)(2,1)S(1)} %pad.14.pick_ref), custom_call_target="tpu_custom_call" | custom-call | tf_op jit(solution)/shard_map/spread_rows/pallas_call | solution.py:505
  69.9 1.3 copy-done.5
  71.2 4.2 reshape.287
  75.4 3.6 convolution_convert_fusion.1
  79.0 4.2 reshape.288.x_ref
  84.5 1.3 reshape.290.extra_ref
  85.8 1.6 copy-done.1
  89.4 158.0 %reduce_rows.1 = (f32[256,3584]{1,0:T(8,128)}, bf16[256,128]{1,0:T(8,128)(2,1)S(1)}) custom-call(bf16[8,256,512]{2,1,0:T(8,128)(2,1)S(1)} %copy-done.1, bf16[512,512]{1,0:T(8,128)(2,1)S(1)} %copy-done.6, bf16[512,512]{1,0:T(8,128)(2,1)S(1)} %copy-done.7, bf16[512,512]{1,0:T(8,128)(2,1)S(1)} %copy-done.8, bf16[512,2048]{1,0:T(8,128)(2,1)} %wf_ref.2, ...), custom_call_target="tpu_custom_call" | custom-call | tf_op jit(solution)/shard_map/reduce_rows/pallas_call | solution.py:263
  247.5 2.1 fusion.16
  249.9 1.6 fusion.124
  252.7 4.0 fusion.37
  257.2 2.1 fusion.20
  260.0 5.0 %fusion.6 = bf16[256,2048]{1,0:T(8,128)(2,1)S(1)} fusion(bf16[1024,2048]{1,0:T(8,128)(2,1)} %param.37, f32[256,3584]{1,0:T(8,128)} %get-tuple-element.15, f32[2048]{0:T(1024)S(1)} %copy-done.14, s32[1024]{0:T(1024)S(1)} %get-tuple-element.28, s32[256]{0:T(256)S(1)} %select_reduce_fusion.1, s32[1024]{0:T(1024)S(1)} %get-tuple-element.27, ...), kind=kOutput, calls=%fused_computation.10 | convolution fusion | flops 1088700416 | bytes 7422976 | tf_op jit(solution)/shard_map/dot_general | solution.py:21
  265.1 1.5 copy-done.4
  266.7 102.4 %gather_multiply.1 = bf16[8,256,512]{2,1,0:T(8,128)(2,1)S(1)} custom-call(bf16[256,2560]{1,0:T(8,128)(2,1)S(1)} %pad_maximum_fusion.act_ref, bf16[512,512]{1,0:T(8,128)(2,1)S(1)} %copy-done.9, bf16[2048,512]{1,0:T(8,128)(2,1)S(1)} %copy-done.4), custom_call_target="tpu_custom_call" | custom-call | tf_op jit(solution)/shard_map/gather_multiply/pallas_call | solution.py:368
  369.1 1.3 copy-done.2
  370.3 4.2 reshape.295
  374.6 3.6 convolution_convert_fusion
  378.2 4.2 reshape.296.y_ref
  382.4 1.6 copy-done.3
  384.0 36.7 %collect_rows.1 = bf16[2,4,64,512]{3,2,1,0:T(8,128)(2,1)S(1)} custom-call(bf16[8,4,64,512]{3,2,1,0:T(8,128)(2,1)S(1)} %copy-done.3), custom_call_target="tpu_custom_call" | custom-call | tf_op jit(solution)/shard_map/collect_rows/pallas_call | solution.py:603
  420.8 1.8 copy.59
  422.6 3.2 reshape.299
  425.8 2.2 add_convert_fusion
  (80 shorter events, 12.2 us)
Async XLA Ops:
  0.0 17.5 %copy-start = (bf16[1024,1024]{1,0:T(8,128)(2,1)S(1)}, bf16[1024,1024]{1,0:T(8,128)(2,1)}, u32[]{:S(2)}) copy-start(bf16[1024,1024]{1,0:T(8,128)(2,1)} %param.30) | copy-start | bytes 6291460
  17.5 2.1 copy-start.10
  69.9 1.3 copy-start.5
  83.2 2.6 copy-start.6
  85.7 1.6 copy-start.1
  87.3 1.0 copy-start.7
  88.4 1.0 copy-start.8
  249.7 2.8 copy-start.12
  259.3 0.7 copy-start.14
  265.0 1.6 copy-start.4
  265.0 1.7 copy-start.9
  369.1 1.3 copy-start.2
  382.4 1.6 copy-start.3
  420.8 5.0 %copy-start.11 = (bf16[32,8,1024]{2,1,0:T(8,128)(2,1)S(1)}, bf16[32,8,1024]{2,1,0:T(8,128)(2,1)}, u32[]{:S(2)}) copy-start(bf16[32,8,1024]{2,1,0:T(8,128)(2,1)} %param.20) | copy-start | bytes 1572868
  420.8 5.0 %copy-start.13 = (f32[1024]{0:T(1024)S(1)}, f32[1024]{0:T(1024)}, u32[]{:S(2)}) copy-start(f32[1024]{0:T(1024)} %param.39) | copy-start | bytes 12292
